TPU v7x, 32 devices: a whole 2x2x4 slice. The times are simulated.
32 devices in a mesh: section: 4 (over x, core), batch: 8 (over z, y).
Axes of the slice: x: 2, y: 2, z: 4, core: 2. Of those that a mesh axis runs over, the one named last changes fastest.
Arguments:
- activations: bfloat16 [16, 1024, 512], P('batch', 'section'), may hold values from -6 to 6
- cotangent: bfloat16 [16, 1024, 512], P('batch', 'section'), may hold values from -6 to 6
- lengths: int32 [16, 8], replicated, may hold values from 0 to 1024, as said below
- gate_weight: bfloat16 [2, 512, 3072], replicated, may hold values from -0.25 to 0.25
- gate_bias: float32 [2, 3072], replicated, may hold values from -12 to 5
- out_weight: bfloat16 [2, 1024, 512], replicated, may hold values from -0.1875 to 0.1875
- up_weight: bfloat16 [2, 512, 2048], replicated, may hold values from -0.25 to 0.25
- down_weight: bfloat16 [2, 2048, 512], replicated, may hold values from -0.125 to 0.125
- mix_gain: float32 [2, 512], replicated, may hold values from 0.25 to 1.75
- mlp_gain: float32 [2, 512], replicated, may hold values from 0.25 to 1.75
Outputs:
- layer_out: float32 [16, 1024, 512], P('batch', 'section')
- input_grad: float32 [16, 1024, 512], P('batch', 'section')
- gate_weight_grad: float32 [2, 512, 3072], P(None, 'section', 'batch')
- gate_bias_grad: float32 [2, 3072], replicated
- out_weight_grad: float32 [2, 1024, 512], P(None, 'section', 'batch')
- up_weight_grad: float32 [2, 512, 2048], P(None, 'section', 'batch')
- down_weight_grad: float32 [2, 2048, 512], P(None, 'section', 'batch')
- mix_gain_grad: float32 [2, 512], replicated
- mlp_gain_grad: float32 [2, 512], replicated
- forget_mean: float32 [2], replicated
Inputs may be any that keep to these rules, and one draw needn't show every extreme that they name: In each sequence the nonzero lengths come first; each is between 128 and 512 and their sum is at most 1024, except that in each aligned block of 2 sequences one sequence holds a single document of 1024 positions.
All inputs are finite; a program needn't handle non-finite values.
Results may differ from a plain program's by a relative error of at most 0.007.
Values sent between devices are 32-bit elements; how exact they have to be, the bound alone decides.
A program may use at most 192 MiB of HBM per device.

v0:
```python
import functools
import types

import jax
import jax.numpy as jnp
from jax import lax
from jax.experimental import pallas as pl
from jax.experimental.pallas import tpu as pltpu
from jax.sharding import PartitionSpec as P

epsilon = 1e-06
MESH = pl.DeviceIdType.MESH
F32, BF16 = jnp.float32, jnp.bfloat16
CHUNKS = 8
LANES = 128
ROOT_HALF = 0.7071067811865476
ROOT_TAU = 0.3989422804014327


def tile(index, size):
    return pl.ds(pl.multiple_of(index * size, size), size)


def inverse(value):
    r = pltpu.reciprocal(value, approx=True)
    return r * (2.0 - value * r)


def normal_below(p):
    return 0.5 + 0.5 * lax.erf(p * ROOT_HALF)


def steps_of(count, unroll, one, start, reverse=False):
    def turn(i, carry):
        for k in range(unroll):
            at = i * unroll + k
            carry = one(count - 1 - at if reverse else at, carry)
        return carry

    return lax.fori_loop(0, count // unroll, turn, start)


def gate_weights(a, b):
    inv = inverse(2.0 + a + b)
    return (1.0 + b) * inv, (1.0 + a) * inv, inv


def greet_section(sections):
    me = lax.axis_index("section")
    barrier = pltpu.get_barrier_semaphore()
    for hop in range(1, sections):
        pl.semaphore_signal(
            barrier, inc=1, device_id={"section": lax.rem(me + hop, sections)}, device_id_type=MESH
        )
    pl.semaphore_wait(barrier, sections - 1)


def exchange(mine, slots, send_sems, recv_sems, sections):
    me = lax.axis_index("section")
    copies = []
    for hop in range(1, sections):
        copies.append(
            pltpu.make_async_remote_copy(
                src_ref=mine,
                dst_ref=slots.at[me],
                send_sem=send_sems.at[hop - 1],
                recv_sem=recv_sems.at[hop - 1],
                device_id={"section": lax.rem(me + hop, sections)},
                device_id_type=MESH,
            )
        )
    for copy in copies:
        copy.start()
    slots[me] = mine[...]
    for copy in copies:
        copy.wait()


def norm_rows(stream, gain, low, rows, step):
    def one(i, carry):
        at = tile(i, step)
        x = stream[at, :]
        r = lax.rsqrt(jnp.mean(x * x, axis=-1, keepdims=True) + epsilon)
        low[at, :] = (x * r * gain[...]).astype(BF16)
        return carry

    lax.fori_loop(0, rows // step, one, 0)


def norm_back(stream, gain, grad, through, out, gain_sum, rows, step):
    width = stream.shape[1]

    def one(i, total):
        at = tile(i, step)
        x = stream[at, :]
        r = lax.rsqrt(jnp.mean(x * x, axis=-1, keepdims=True) + epsilon)
        n = x * r
        g = grad[at, :]
        a = g * gain[...]
        out[at, :] = through[at, :] + r * (a - n * jnp.mean(a * n, axis=-1, keepdims=True))
        return total + jnp.sum((g * n).reshape(step // 8, 8, width), axis=0)

    gain_sum[...] = lax.fori_loop(0, rows // step, one, jnp.zeros((8, width), F32))


def fill_masks(lens, valid, keep, sizes, turned=False):
    section = lax.axis_index("section")
    group = lax.axis_index("batch")
    starts, totals = [], []
    for s in range(sizes.micro):
        total, begin = 0, []
        for d in range(lens.shape[0 if turned else 1]):
            row = group * sizes.micro + s
            length = lens[d, row] if turned else lens[row, d]
            begin.append(jnp.where(length > 0, total, -1))
            total = total + length
        starts.append(begin)
        totals.append(total)
    chunk_place = lax.broadcasted_iota(jnp.int32, (8, LANES), 0) * sizes.steps

    def one(j, carry):
        for s in range(sizes.micro):
            place = section * sizes.span + j + chunk_place
            true = place < totals[s]
            first = place == starts[s][0]
            for begin in starts[s][1:]:
                first = first | (place == begin)
            at = pl.ds(pl.multiple_of(j * sizes.group + s * 8, 8), 8)
            valid[at, :] = jnp.where(true, 1.0, 0.0)
            keep[at, :] = jnp.where(true & jnp.logical_not(first), 1.0, 0.0)
        return carry

    lax.fori_loop(0, sizes.steps, one, 0)


def scan_totals(first, second, sizes, reverse, prefix, chunk, mine):
    for s in range(sizes.micro):
        p = jnp.ones((1, sizes.hidden), F32)
        t = jnp.zeros((1, sizes.hidden), F32)
        for c in reversed(range(CHUNKS)) if reverse else range(CHUNKS):
            at = s * 8 + c
            prefix[0, at : at + 1, :] = p
            prefix[1, at : at + 1, :] = t
            pc = first[at : at + 1, :]
            t = pc * t + second[at : at + 1, :]
            p = p * pc
        mine[s : s + 1, :] = p
        mine[sizes.micro + s : sizes.micro + s + 1, :] = t


def scan_enter(slots, prefix, enter, sizes, reverse):
    me = lax.axis_index("section")
    for s in range(sizes.micro):
        a = jnp.zeros((1, sizes.hidden), F32)
        order = range(sizes.sections - 1, 0, -1) if reverse else range(sizes.sections - 1)
        for k in order:
            reached = k > me if reverse else k < me
            pk = slots[k, s : s + 1, :]
            tk = slots[k, sizes.micro + s : sizes.micro + s + 1, :]
            a = jnp.where(reached, pk * a + tk, a)
        at = slice(s * 8, s * 8 + 8)
        enter[at, :] = prefix[0, at, :] * a + prefix[1, at, :]


class Sizes:
    def __init__(self, micro, span, width, hidden, inner, sections):
        self.micro, self.span, self.width = micro, span, width
        self.hidden, self.inner, self.sections = hidden, inner, sections
        self.rows = micro * span
        self.steps = span // CHUNKS
        self.group = micro * CHUNKS


def forward_kernel(
    sizes,
    layer,
    stream,
    valid,
    keep,
    bias,
    mix_gain,
    mlp_gain,
    gate_hbm,
    out_hbm,
    up_hbm,
    down_hbm,
    next_stream,
    u,
    sf_out,
    si_out,
    zc_out,
    states,
    y1,
    v,
    p_out,
    gb,
    forget,
    pair_slots,
    gate_w,
    out_w,
    up_w,
    down_w,
    z,
    decay,
    drive,
    hb,
    chunk_p,
    chunk_t,
    prefix,
    enter,
    mine,
    weight_sems,
    send_sems,
    recv_sems,
):
    sz = sizes
    loads = [
        pltpu.make_async_copy(src.at[layer], dst, weight_sems.at[i])
        for i, (src, dst) in enumerate(
            ((gate_hbm, gate_w), (out_hbm, out_w), (up_hbm, up_w), (down_hbm, down_w))
        )
    ]
    for load in loads:
        load.start()
    greet_section(sz.sections)
    mine[...] = jnp.zeros_like(mine)
    norm_rows(stream, mix_gain, u, sz.rows, 64)
    loads[0].wait()
    forget[...] = jnp.zeros_like(forget)
    hw = 256

    def gate_tile(n, carry):
        for part in range(3):
            cols = pl.ds(pl.multiple_of(part * sz.hidden + n * hw, hw), hw)
            z[:, part * hw : (part + 1) * hw] = (
                jnp.dot(u[...], gate_w[:, cols], preferred_element_type=F32) + bias[:, cols]
            )

        def one(i, inner):
            at = tile(i, 64)
            for lane in range(hw // LANES):
                src = lambda part: z[
                    at, part * hw + lane * LANES : part * hw + (lane + 1) * LANES
                ]
                dst = pl.ds(pl.multiple_of(n * hw + lane * LANES, LANES), LANES)
                a = jnp.exp(jnp.minimum(-src(0), 86.0))
                b = jnp.exp(jnp.minimum(-src(1), 86.0))
                zc = src(2)
                fp, ip, _ = gate_weights(a, b)
                vm = valid[at, :]
                decay[at, dst] = fp * keep[at, :]
                drive[at, dst] = ip * zc * vm
                sf_out[at, dst] = a
                si_out[at, dst] = b
                zc_out[at, dst] = zc
                forget[...] += jnp.sum((fp * vm).reshape(8, 8, LANES), axis=0)
            return inner

        lax.fori_loop(0, sz.rows // 64, one, 0)
        return carry

    lax.fori_loop(0, sz.hidden // hw, gate_tile, 0)
    half = sz.hidden // 2
    for part in range(2):
        lanes = slice(part * half, (part + 1) * half)

        def totals(j, pair):
            at = tile(j, sz.group)
            d = decay[at, lanes]
            return pair[0] * d, pair[1] * d + drive[at, lanes]

        one = jnp.ones((sz.group, half), F32)
        pair = steps_of(sz.steps, 4, totals, (one, jnp.zeros_like(one)))
        chunk_p[:, lanes] = pair[0]
        chunk_t[:, lanes] = pair[1]
    scan_totals(chunk_p, chunk_t, sz, False, prefix, None, mine)
    exchange(mine, pair_slots, send_sems, recv_sems, sz.sections)
    scan_enter(pair_slots, prefix, enter, sz, False)
    states[0 : sz.group, :] = enter[...]
    for part in range(2):
        lanes = slice(part * half, (part + 1) * half)

        def walk(j, h):
            at = tile(j, sz.group)
            h = decay[at, lanes] * h + drive[at, lanes]
            states[tile(j + 1, sz.group), lanes] = h
            hb[at, lanes] = h.astype(BF16)
            return h

        steps_of(sz.steps, 4, walk, enter[:, lanes])
    loads[1].wait()

    def out_tile(n, carry):
        cols = tile(n, 256)
        y1[:, cols] = stream[:, cols] + jnp.dot(
            hb[...], out_w[:, cols], preferred_element_type=F32
        )
        return carry

    lax.fori_loop(0, sz.width // 256, out_tile, 0)
    norm_rows(y1, mlp_gain, v, sz.rows, 64)
    loads[2].wait()

    def up_tile(n, carry):
        cols = tile(n, 256)
        p_out[:, cols] = jnp.dot(v[...], up_w[:, cols], preferred_element_type=F32)

        def one(i, inner):
            at = tile(i, 64)
            p = p_out[at, cols]
            gb[at, cols] = (p * normal_below(p)).astype(BF16)
            return inner

        lax.fori_loop(0, sz.rows // 64, one, 0)
        return carry

    lax.fori_loop(0, sz.inner // 256, up_tile, 0)
    loads[3].wait()

    def down_tile(n, carry):
        cols = tile(n, 256)
        next_stream[:, cols] = y1[:, cols] + jnp.dot(
            gb[...], down_w[:, cols], preferred_element_type=F32
        )
        return carry

    lax.fori_loop(0, sz.width // 256, down_tile, 0)


def backward_kernel(
    sizes,
    layer,
    gx,
    stream,
    valid,
    keep,
    mix_gain,
    mlp_gain,
    u,
    sf_in,
    si_in,
    zc_in,
    states,
    y1,
    v,
    p_in,
    gb,
    pair_slots,
    gate_hbm,
    out_hbm,
    up_hbm,
    down_hbm,
    next_gx,
    gate_grad,
    out_grad,
    up_grad,
    down_grad,
    bias_sum,
    mix_sum,
    mlp_sum,
    gate_w,
    out_w,
    up_w,
    down_w,
    low,
    low_t,
    wide_t,
    hb,
    ga,
    gp,
    gz,
    grad,
    gy1,
    decay,
    chunk_p,
    chunk_t,
    prefix,
    enter,
    mine,
    slots,
    weight_sems,
    send_sems,
    recv_sems,
):
    sz = sizes
    loads = [
        pltpu.make_async_copy(src.at[layer], dst, weight_sems.at[i])
        for i, (src, dst) in enumerate(
            ((gate_hbm, gate_w), (out_hbm, out_w), (up_hbm, up_w), (down_hbm, down_w))
        )
    ]
    for load in reversed(loads):
        load.start()
    greet_section(sz.sections)
    mine[...] = jnp.zeros_like(mine)

    def cast(i, carry):
        at = tile(i, 64)
        low[at, :] = gx[at, :].astype(BF16)
        return carry

    lax.fori_loop(0, sz.rows // 64, cast, 0)
    low_t[...] = low[...].T

    def weight_grad(left_t, right, dst, step):
        def one(n, carry):
            cols = tile(n, step)
            dst[:, cols] = jnp.dot(left_t[...], right[:, cols], preferred_element_type=F32)
            return carry

        lax.fori_loop(0, right.shape[1] // step, one, 0)

    weight_grad(low_t, gb, down_grad, 256)
    loads[3].wait()

    def act_tile(n, carry):
        cols = tile(n, 256)
        ga[:, :256] = lax.dot_general(
            low[...], down_w[cols, :], (((1,), (1,)), ((), ())), preferred_element_type=F32
        )

        def one(i, inner):
            at = tile(i, 64)
            p = p_in[at, cols]
            slope = normal_below(p) + ROOT_TAU * p * jnp.exp(-0.5 * p * p)
            gp[at, cols] = (ga[at, :256] * slope).astype(BF16)
            return inner

        lax.fori_loop(0, sz.rows // 64, one, 0)
        return carry

    lax.fori_loop(0, sz.inner // 256, act_tile, 0)
    wide_t[...] = v[...].T
    weight_grad(wide_t, gp, up_grad, 256)
    loads[2].wait()

    def contract(left, weight, dst, step):
        def one(n, carry):
            cols = tile(n, step)
            dst[:, cols] = lax.dot_general(
                left[...], weight[cols, :], (((1,), (1,)), ((), ())), preferred_element_type=F32
            )
            return carry

        lax.fori_loop(0, weight.shape[0] // step, one, 0)

    contract(gp, up_w, grad, 256)
    norm_back(y1, mlp_gain, grad, gx, gy1, mlp_sum, sz.rows, 64)

    def cast_more(i, carry):
        at = tile(i, 64)
        low[at, :] = gy1[at, :].astype(BF16)
        return carry

    lax.fori_loop(0, sz.rows // 64, cast_more, 0)

    def cast_state(i, carry):
        hb[tile(i, sz.group), :] = states[tile(i + 1, sz.group), :].astype(BF16)
        return carry

    lax.fori_loop(0, sz.steps, cast_state, 0)
    low_t[...] = low[...].T
    weight_grad(low_t, hb, out_grad, 256)
    loads[1].wait()
    contract(low, out_w, ga, 256)
    half = sz.hidden // 2
    for part in range(2):
        lanes = slice(part * half, (part + 1) * half)

        def totals(i, pair):
            at = tile(sz.steps - 1 - i, sz.group)
            mask = jnp.concatenate([keep[at, :]] * (half // LANES), axis=1)
            d = gate_weights(sf_in[at, lanes], si_in[at, lanes])[0] * mask
            decay[at, lanes] = d
            return pair[0] * d, d * (ga[at, lanes] + pair[1])

        pair = lax.fori_loop(
            0,
            sz.steps,
            totals,
            (jnp.ones((sz.group, half), F32), jnp.zeros((sz.group, half), F32)),
        )
        chunk_p[:, lanes] = pair[0]
        chunk_t[:, lanes] = pair[1]
    scan_totals(chunk_p, chunk_t, sz, True, prefix, None, mine)
    exchange(mine, slots, send_sems, recv_sems, sz.sections)
    scan_enter(slots, prefix, enter, sz, True)

    def gate_lane(n, carry):
        lanes = tile(n, LANES)

        def walk(i, kept):
            m, bf, bi, bc = kept
            j = sz.steps - 1 - i
            at = tile(j, sz.group)
            d = decay[at, lanes]
            q = ga[at, lanes] + m
            a = sf_in[at, lanes]
            b = si_in[at, lanes]
            zc = zc_in[at, lanes]
            vm = valid[at, :]
            fp, ip, inv = gate_weights(a, b)
            gf = q * (states[at, lanes] * keep[at, :] - zc * vm)
            gzf = (gf * (a * inv) * fp).astype(BF16)
            gzi = (-gf * (b * inv) * ip).astype(BF16)
            gzc = (q * vm * ip).astype(BF16)
            gz[at, lanes] = gzf
            gz[at, pl.ds(pl.multiple_of(sz.hidden + n * LANES, LANES), LANES)] = gzi
            gz[at, pl.ds(pl.multiple_of(2 * sz.hidden + n * LANES, LANES), LANES)] = gzc
            return (
                d * q,
                bf + gzf.astype(F32),
                bi + gzi.astype(F32),
                bc + gzc.astype(F32),
            )

        zero = jnp.zeros((sz.group, LANES), F32)
        _, bf, bi, bc = lax.fori_loop(0, sz.steps, walk, (enter[:, lanes], zero, zero, zero))
        for part, total in enumerate((bf, bi, bc)):
            where = pl.ds(pl.multiple_of(part * sz.hidden + n * LANES, LANES), LANES)
            bias_sum[:, where] = jnp.sum(total.reshape(sz.group // 8, 8, LANES), axis=0)
        return carry

    lax.fori_loop(0, sz.hidden // LANES, gate_lane, 0)
    wide_t[...] = u[...].T
    weight_grad(wide_t, gz, gate_grad, 256)
    loads[0].wait()
    contract(gz, gate_w, grad, 256)
    norm_back(stream, mix_gain, grad, gy1, next_gx, mix_sum, sz.rows, 64)


VMEM = pl.BlockSpec(memory_space=pltpu.VMEM)
ANY = pl.BlockSpec(memory_space=pl.ANY)
LIMIT = 62 * 2**20


def shape(*dims, kind=F32):
    return jax.ShapeDtypeStruct(dims, kind)


def exchange_scratch(sz):
    return [
        pltpu.SemaphoreType.DMA((4,)),
        pltpu.SemaphoreType.DMA((sz.sections - 1,)),
        pltpu.SemaphoreType.DMA((sz.sections - 1,)),
    ]


def weight_scratch(sz):
    return [
        pltpu.VMEM((sz.width, 3 * sz.hidden), BF16),
        pltpu.VMEM((sz.hidden, sz.width), BF16),
        pltpu.VMEM((sz.width, sz.inner), BF16),
        pltpu.VMEM((sz.inner, sz.width), BF16),
    ]


def scan_scratch(sz):
    return [
        pltpu.VMEM((sz.group, sz.hidden), F32),
        pltpu.VMEM((sz.group, sz.hidden), F32),
        pltpu.VMEM((2, sz.group, sz.hidden), F32),
        pltpu.VMEM((sz.group, sz.hidden), F32),
        pltpu.VMEM((8, sz.hidden), F32),
    ]


def run_forward(sz, layer, stream, masks, bias, mix_gain, mlp_gain, weights):
    r, d, h, f = sz.rows, sz.width, sz.hidden, sz.inner
    return pl.pallas_call(
        functools.partial(forward_kernel, sz, layer),
        out_shape=(
            shape(r, d),
            shape(r, d, kind=BF16),
            shape(r, h),
            shape(r, h),
            shape(r, h),
            shape(r + sz.group, h),
            shape(r, d),
            shape(r, d, kind=BF16),
            shape(r, f),
            shape(r, f, kind=BF16),
            shape(8, LANES),
            shape(sz.sections, 8, h),
        ),
        in_specs=[VMEM] * 6 + [ANY] * 4,
        out_specs=[VMEM] * 12,
        scratch_shapes=weight_scratch(sz)
        + [
            pltpu.VMEM((r, 3 * 256), F32),
            pltpu.VMEM((r, h), F32),
            pltpu.VMEM((r, h), F32),
            pltpu.VMEM((r, h), BF16),
        ]
        + scan_scratch(sz)
        + exchange_scratch(sz),
        compiler_params=pltpu.CompilerParams(
            collective_id=layer, has_side_effects=True, vmem_limit_bytes=LIMIT
        ),
        name=f"forward_{layer}",
    )(stream, *masks, bias, mix_gain, mlp_gain, *weights)


def run_backward(sz, layer, gx, stream, masks, mix_gain, mlp_gain, saved, weights):
    r, d, h, f = sz.rows, sz.width, sz.hidden, sz.inner
    return pl.pallas_call(
        functools.partial(backward_kernel, sz, layer),
        out_shape=(
            shape(r, d),
            shape(d, 3 * h),
            shape(d, h),
            shape(d, f),
            shape(d, f),
            shape(8, 3 * h),
            shape(8, d),
            shape(8, d),
        ),
        in_specs=[VMEM] * 16 + [ANY] * 4,
        out_specs=[VMEM] * 8,
        scratch_shapes=weight_scratch(sz)
        + [
            pltpu.VMEM((r, d), BF16),
            pltpu.VMEM((d, r), BF16),
            pltpu.VMEM((d, r), BF16),
            pltpu.VMEM((r, h), BF16),
            pltpu.VMEM((r, h), F32),
            pltpu.VMEM((r, f), BF16),
            pltpu.VMEM((r, 3 * h), BF16),
            pltpu.VMEM((r, d), F32),
            pltpu.VMEM((r, d), F32),
            pltpu.VMEM((r, h), F32),
        ]
        + scan_scratch(sz)
        + [pltpu.VMEM((sz.sections, 8, h), F32)]
        + exchange_scratch(sz),
        compiler_params=pltpu.CompilerParams(
            collective_id=2 + layer, has_side_effects=True, vmem_limit_bytes=LIMIT
        ),
        name=f"backward_{layer}",
    )(gx, stream, *masks, mix_gain, mlp_gain, *saved, *weights)


BLOCK = 64
HELD = 3
RINGS = (4, 5, 5, 5, 5)
SENDS = 8
STAGES = 5
WINDOW = 4
SMALL = 1280


class Units:
    def __init__(self, count, refs):
        self.count = count
        self.__dict__.update(vars(refs))
        self.arrived = [getattr(refs, f"arrived{stage}") for stage in range(STAGES)]
        section, batch = lax.axis_index("section"), lax.axis_index("batch")
        core, x = section % 2, section // 2
        y, za, zb = batch % 2, (batch // 2) % 2, batch // 4
        self.core = core
        self.bits = ((x, za, y, zb), (y, za, x, zb))
        self.names = (("x", "za", "y", "zb"), ("y", "za", "x", "zb"))
        self.partner = {
            "core": {"section": section + 1 - 2 * core},
            "x": {"section": section + 2 - 4 * x},
            "y": {"batch": batch + 1 - 2 * y},
            "za": {"batch": batch + 2 - 4 * za},
            "zb": {"batch": batch + 4 - 8 * zb},
        }
        self.now = 0.0
        self.links = ("core", "x", "y", "z")
        self.free_at = dict.fromkeys(self.links, 0.0)
        self.flying = dict.fromkeys(self.links, 0)
        self.queues = {link: [] for link in self.links}
        self.ready = {}
        self.summed = set()
        self.copies = {}
        self.small_left = None

    def greet(self):
        barrier = pltpu.get_barrier_semaphore()
        section = lax.axis_index("section")
        others = [self.partner["y"], self.partner["za"], self.partner["zb"]]
        others += [{"section": lax.rem(section + hop, 4)} for hop in range(1, 4)]
        for other in others:
            pl.semaphore_signal(barrier, inc=1, device_id=other, device_id_type=MESH)
        pl.semaphore_wait(barrier, len(others))

    def name(self, stage, half):
        return "core" if stage == 0 else self.names[half][stage - 1]

    def link(self, stage, half):
        name = self.name(stage, half)
        return "z" if name[0] == "z" else name

    def arrival(self, unit, stage, half):
        ref = self.arrived[stage].at[unit % RINGS[stage]]
        return ref if stage == 0 else ref.at[half]

    def copy(self, unit, stage, half):
        at = 0 if stage == 0 else 2 * stage - 1 + half
        if stage == 0:
            src = self.held.at[unit % HELD, 1 - self.core]
        else:
            count = 16 >> stage
            src = self.arrived[stage - 1].at[unit % RINGS[stage - 1], half]
            src = src.at[pl.ds((1 - self.bits[half][stage - 1]) * count, count)]
        return pltpu.make_async_remote_copy(
            src_ref=src,
            dst_ref=self.arrival(unit, stage, half),
            send_sem=self.send_sems.at[unit % SENDS, at],
            recv_sem=self.recv_sems.at[unit % RINGS[stage], at],
            device_id=self.partner[self.name(stage, half)],
            device_id_type=MESH,
        )

    def has_place(self, unit, stage, half):
        before = unit - RINGS[stage]
        if before < 0:
            return True
        if stage == 0:
            return (before, 1, 0) in self.summed and (before, 1, 1) in self.summed
        return (before, min(stage + 1, STAGES - 1), half) in self.summed

    def credit(self, unit, stage, half):
        if unit + RINGS[stage] < self.count:
            pl.semaphore_signal(
                self.credits.at[0 if stage == 0 else 2 * stage - 1 + half],
                inc=1,
                device_id=self.partner[self.name(stage, half)],
                device_id_type=MESH,
            )

    def pump(self):
        for link, queue in self.queues.items():
            while self.flying[link] < WINDOW:
                key = next((key for key in queue if self.has_place(*key)), None)
                if key is None:
                    break
                queue.remove(key)
                self.flying[link] += 1
                unit, stage, half = key
                if unit >= RINGS[stage]:
                    at = 0 if stage == 0 else 2 * stage - 1 + half
                    pl.semaphore_wait(self.credits.at[at], 1)
                self.copies[key] = self.copy(*key)
                self.copies[key].start()
                size = (32 if stage == 0 else 16 >> stage) * BLOCK * LANES * 4
                rate = 250e3 if link == "core" else 45e3
                self.free_at[link] = max(self.now, self.free_at[link]) + size / rate
                self.ready[key] = self.free_at[link] + 1.5

    def push(self, unit, stage, half):
        self.queues[self.link(stage, half)].append((unit, stage, half))
        self.pump()

    def produced(self, *which):
        for unit in which:
            self.push(unit, 0, 0)

    def add(self, dst, src, count):
        turn = min(count, 4)

        def one(i, carry):
            for k in range(turn):
                dst[i * turn + k] += src[i * turn + k]
            return carry

        if count == turn:
            one(0, 0)
        else:
            lax.fori_loop(0, count // turn, one, 0)

    def step(self, unit, stage, half):
        key = (unit, stage, half)
        del self.ready[key]
        assert unit == 0 or (unit - 1, stage, half) in self.summed
        self.copies[key].wait_recv()
        here = self.arrival(unit, stage, half)
        if stage == 0:
            for h in range(2):
                self.add(here.at[h], self.held.at[unit % HELD, self.core, h], 16)
        else:
            count = 16 >> stage
            before = self.arrived[stage - 1].at[unit % RINGS[stage - 1], half]
            self.add(here, before.at[pl.ds(self.bits[half][stage - 1] * count, count)], count)
            self.copies.pop(key).wait_send()
        self.summed.add(key)
        self.flying[self.link(stage, half)] -= 1
        self.now += 0.25
        if stage > 1 or (unit, 1, 1 - half) in self.summed:
            if stage > 0:
                self.credit(unit, stage - 1, half if stage > 1 else 0)
        if stage == 0:
            for h in range(2):
                self.push(unit, 1, h)
        elif stage < STAGES - 1:
            self.push(unit, stage + 1, half)
        else:
            self.finish(unit, half, here[0])
            self.credit(unit, stage, half)
        self.pump()

    def finish(self, unit, half, block):
        layer, k = self.count // 8 - 1 - unit // 8, unit % 8
        if k < 2 or k == 4:
            ref, at = (self.down_weight_grad, k) if k < 2 else (self.out_weight_grad, 0)
            ref[layer, :, at * 256 + half * 128 : at * 256 + half * 128 + 128] = block
        else:
            ref, at = (self.up_weight_grad, k - 2) if k < 4 else (self.gate_weight_grad, k - 5)
            rows = slice(half * BLOCK, half * BLOCK + BLOCK)
            ref[layer, rows, at * LANES : at * LANES + LANES] = block

    def small_copy(self, stage):
        name = ("core", "x", "y", "za", "zb")[stage]
        return pltpu.make_async_remote_copy(
            src_ref=self.small.at[stage],
            dst_ref=self.small_arrived.at[stage],
            send_sem=self.small_send.at[stage],
            recv_sem=self.small_recv.at[stage],
            device_id=self.partner[name],
            device_id_type=MESH,
        )

    def small_start(self):
        self.small_left = 0
        self.small_copies = [self.small_copy(0)]
        self.small_copies[0].start()
        self.small_ready = self.now + 3.0

    def small_step(self):
        stage = self.small_left
        self.small_copies[stage].wait_recv()
        self.small[stage + 1] = self.small[stage] + self.small_arrived[stage]
        self.small_left += 1
        if self.small_left < STAGES:
            self.small_copies.append(self.small_copy(self.small_left))
            self.small_copies[-1].start()
            self.small_ready = self.now + 3.0
        else:
            for copy in self.small_copies:
                copy.wait_send()

    def open(self, unit, stage, half):
        halves = range(2) if stage == 0 else (half,)
        before = unit - RING
        return (
            before < 0
            or stage == STAGES - 1
            or all((before, stage + 1, h) in self.consumed for h in halves)
        )

    def next(self):
        best = min(self.ready.items(), key=lambda item: (item[1], item[0]), default=None)
        small = self.small_left is not None and self.small_left < STAGES
        if small and (best is None or self.small_ready <= best[1]):
            return self.small_ready, None
        return (best[1], best[0]) if best else None

    def take(self, item):
        self.now = max(self.now, item[0])
        if item[1] is None:
            self.small_step()
        else:
            self.step(*item[1])

    def passed(self, us):
        self.now += us
        while (item := self.next()) and item[0] <= self.now:
            self.take(item)

    def room(self, unit):
        before = (unit - HELD, 0, 0)
        while unit >= HELD and before not in self.summed:
            self.take(self.next())
        if before in self.copies:
            self.copies.pop(before).wait_send()

    def drain(self):
        while item := self.next():
            self.take(item)
        for key in list(self.copies):
            self.copies.pop(key).wait_send()


def place(half, x, y, za, zb):
    return (x * 8 + za * 4 + y * 2 + zb) if half == 0 else (y * 8 + za * 4 + x * 2 + zb)


def strided(start, steps):
    return pl.ds(start, CHUNKS, stride=steps)


def whole_step(sz, layers, names, *args):
    r = types.SimpleNamespace(**dict(zip(names, args)))
    units = Units(8 * layers, r)
    valid, keep, low, low_t, wide_t = r.valid, r.keep, r.low, r.low_t, r.wide_t
    hb, ga, gz, grad, gy1, gx = r.hb, r.ga, r.gz, r.grad, r.gy1, r.gx
    gp = gz.at[:, : sz.inner]
    decay, enter, prefix, mine = r.decay, r.enter, r.prefix, r.mine
    small, held = r.small, r.held
    natural = r.natural
    last = layers - 1
    half = sz.hidden // 2
    drive = r.p.at[:, : sz.hidden]
    homes = dict(gate_w=r.gate_hbm, out_w=r.out_hbm, up_w=r.up_hbm, down_w=r.down_hbm)
    homes.update(u=r.u_save, a=r.a_save, b=r.b_save, zc=r.zc_save, states=r.states_save)
    homes.update(y1=r.y1_save, v=r.v_save, p=r.p_save, gb=r.gb_save, stream=r.stream_save)
    keys = types.SimpleNamespace(**{name: name for name in homes})
    index_of = {name: i for i, name in enumerate(homes)}
    loads, saves = {}, {}

    def load(layer, name):
        copy = pltpu.make_async_copy(
            homes[name].at[layer], getattr(r, name), r.load_sems.at[index_of[name]]
        )
        copy.start()
        loads[name] = copy

    def need(*wanted):
        for name in wanted:
            if name in loads:
                loads.pop(name).wait()

    def save(layer, name, ref=None):
        if layer < last:
            src = getattr(r, name) if ref is None else ref
            copy = pltpu.make_async_copy(
                src, homes[name].at[layer], r.save_sems.at[index_of[name]]
            )
            copy.start()
            saves[name] = copy

    def settled(*which):
        for name in which:
            if name in saves:
                saves.pop(name).wait()

    def over(count, one):
        def each(i, carry):
            one(i)
            return carry

        lax.fori_loop(0, count, each, 0)

    act_load = pltpu.make_async_copy(r.activations, hb.at[:, : sz.width], r.in_sems.at[0])
    cot_load = pltpu.make_async_copy(r.cotangent, wide_t, r.in_sems.at[1])
    len_load = pltpu.make_async_copy(r.lengths, r.lens, r.in_sems.at[2])
    len_load.start()
    act_load.start()
    for name in (keys.gate_w, keys.out_w, keys.up_w, keys.down_w):
        load(0, name)
    cot_load.start()
    units.greet()
    mine[...] = jnp.zeros_like(mine)
    small[0] = jnp.zeros((8, SMALL), F32)
    len_load.wait()
    fill_masks(r.lens, valid, keep, sz, True)

    def to_steps(src, put):
        def cast(i):
            at = tile(i, 64)
            for k in range(sz.width // LANES):
                natural[k, at, :] = src[at, k * LANES : (k + 1) * LANES].astype(F32)

        over(sz.rows // 64, cast)

        def gather(j):
            for k in range(sz.width // LANES):
                parts = [
                    natural[k, strided(s * sz.span + j, sz.steps), :] for s in range(sz.micro)
                ]
                put(tile(j, sz.group), slice(k * LANES, (k + 1) * LANES), jnp.concatenate(parts, axis=0))

        over(sz.steps, gather)

    def from_steps(src, dst, sem):
        def scatter(j):
            for k in range(sz.width // LANES):
                value = src[tile(j, sz.group), k * LANES : (k + 1) * LANES]
                for s in range(sz.micro):
                    natural[k, strided(s * sz.span + j, sz.steps), :] = value[s * 8 : s * 8 + 8]

        over(sz.steps, scatter)
        copies = []
        for k in range(sz.width // LANES):
            lanes = slice(k * LANES, (k + 1) * LANES)
            copies.append(pltpu.make_async_copy(natural.at[k], dst.at[:, lanes], sem.at[k]))
            copies[-1].start()
        return copies

    act_load.wait()

    def put_gx(at, lanes, value):
        gx[at, lanes] = value

    to_steps(hb.at[:, : sz.width], put_gx)

    def exchange_start(way, layer):
        slots = r.slots.at[way, layer]
        me = lax.axis_index("section")
        copies = []
        for hop in range(1, sz.sections):
            copies.append(
                pltpu.make_async_remote_copy(
                    src_ref=mine,
                    dst_ref=slots.at[me],
                    send_sem=r.pair_send.at[way, layer, hop - 1],
                    recv_sem=r.pair_recv.at[way, layer, hop - 1],
                    device_id={"section": lax.rem(me + hop, sz.sections)},
                    device_id_type=MESH,
                )
            )
        for copy in copies:
            copy.start()
        slots[me] = mine[...]
        return slots, copies

    def exchange_end(slots, copies, reverse):
        for copy in copies:
            copy.wait()
        scan_enter(slots, prefix, enter, sz, reverse)

    def keep_cotangent():
        cot_load.wait()

        def put_low(at, lanes, value):
            low[at, lanes] = value.astype(BF16)

        to_steps(wide_t, put_low)
        low_t[...] = low[...].T

    def forward(layer):
        stream = r.stream if layer > 0 else gx
        settled(keys.u)
        norm_rows(stream, r.mix_gain.at[layer : layer + 1], r.u, sz.rows, 64)
        save(layer, keys.u)
        if layer == 0:
            save(layer, keys.stream, gx)
        need(keys.gate_w)
        settled(keys.a, keys.b, keys.zc, keys.p)
        hw = 256
        bias = r.gate_bias

        def gate_tile(n, forget):
            for part in range(3):
                cols = pl.ds(pl.multiple_of(part * sz.hidden + n * hw, hw), hw)
                ga[:, part * hw : (part + 1) * hw] = (
                    jnp.dot(r.u[...], r.gate_w[:, cols], preferred_element_type=F32)
                    + bias[layer : layer + 1, cols]
                )
            return lax.fori_loop(0, sz.rows // 64, functools.partial(gate_rows, n), forget)

        def gate_rows(n, i, forget):
            at = tile(i, 64)
            vm, km = valid[at, :], keep[at, :]
            for lane in range(hw // LANES):
                zf, zi, zc = (
                    ga[at, part * hw + lane * LANES : part * hw + (lane + 1) * LANES]
                    for part in range(3)
                )
                dst = pl.ds(pl.multiple_of(n * hw + lane * LANES, LANES), LANES)
                a = jnp.exp(jnp.minimum(-zf, 86.0))
                b = jnp.exp(jnp.minimum(-zi, 86.0))
                fp, ip, _ = gate_weights(a, b)
                decay[at, dst] = fp * km
                drive[at, dst] = ip * zc * vm
                r.a[at, dst] = a
                r.b[at, dst] = b
                r.zc[at, dst] = zc
                forget = forget + jnp.sum((fp * vm).reshape(8, 8, LANES), axis=0)
            return forget

        forget = lax.fori_loop(0, sz.hidden // hw, gate_tile, jnp.zeros((8, LANES), F32))
        small[0, layer * 4 : layer * 4 + 1, sz.hidden : sz.hidden + LANES] = jnp.sum(
            forget, axis=0, keepdims=True
        )
        for name in (keys.a, keys.b, keys.zc):
            save(layer, name)
        if layer < last:
            load(layer + 1, keys.gate_w)
        for part in range(2):
            lanes = slice(part * half, (part + 1) * half)

            def totals(j, pair):
                at = tile(j, sz.group)
                d = decay[at, lanes]
                return pair[0] * d, pair[1] * d + drive[at, lanes]

            one = jnp.ones((sz.group, half), F32)
            pair = steps_of(sz.steps, 2, totals, (one, jnp.zeros_like(one)))
            r.chunk_p[:, lanes] = pair[0]
            r.chunk_t[:, lanes] = pair[1]
        scan_totals(r.chunk_p, r.chunk_t, sz, False, prefix, None, mine)
        flight = exchange_start(0, layer)
        settled(keys.states, keys.y1, keys.v, keys.gb, keys.stream)
        exchange_end(*flight, False)
        states = r.states
        states[0 : sz.group, :] = enter[...]
        for part in range(2):
            lanes = slice(part * half, (part + 1) * half)

            def walk(j, h):
                at = tile(j, sz.group)
                h = decay[at, lanes] * h + drive[at, lanes]
                states[tile(j + 1, sz.group), lanes] = h
                hb[at, lanes] = h.astype(BF16)
                return h

            steps_of(sz.steps, 4, walk, enter[:, lanes])
        save(layer, keys.states)
        need(keys.out_w)

        def out_tile(n):
            cols = tile(n, 256)
            r.y1[:, cols] = stream[:, cols] + jnp.dot(
                hb[...], r.out_w[:, cols], preferred_element_type=F32
            )

        over(sz.width // 256, out_tile)
        save(layer, keys.y1)
        if layer < last:
            load(layer + 1, keys.out_w)
        norm_rows(r.y1, r.mlp_gain.at[layer : layer + 1], r.v, sz.rows, 64)
        save(layer, keys.v)
        need(keys.up_w)

        def up_tile(n):
            cols = tile(n, 256)
            r.p[:, cols] = jnp.dot(r.v[...], r.up_w[:, cols], preferred_element_type=F32)

            def one(i):
                at = tile(i, 64)
                p = r.p[at, cols]
                r.gb[at, cols] = (p * normal_below(p)).astype(BF16)

            over(sz.rows // 64, one)

        over(sz.inner // 256, up_tile)
        save(layer, keys.p)
        save(layer, keys.gb)
        if layer < last:
            load(layer + 1, keys.up_w)
        else:
            down_grad(layer, 0)
        need(keys.down_w)
        out = r.stream if layer < last else gy1

        def down_tile(n):
            cols = tile(n, 256)
            out[:, cols] = r.y1[:, cols] + jnp.dot(
                r.gb[...], r.down_w[:, cols], preferred_element_type=F32
            )

        over(sz.width // 256, down_tile)
        if layer < last:
            load(layer + 1, keys.down_w)

    def down_grad(layer, unit):
        for k in range(2):
            units.room(unit + k)

        def one(n):
            s, t = n // 2, n % 2
            value = jnp.dot(low_t[...], r.gb[:, tile(n, 256)], preferred_element_type=F32)
            for b in range(8):
                for h in range(2):
                    at = place(h, s // 2, b % 2, (b // 2) % 2, b // 4)
                    held[(unit + t) % HELD, s % 2, h, at] = value[
                        b * 64 : b * 64 + 64, h * 128 : h * 128 + 128
                    ]

        over(8, one)
        units.produced(unit, unit + 1)
        units.passed(3)

    def cast(src, dst):
        def one(i):
            at = tile(i, 64)
            dst[at, :] = src[at, :].astype(dst.dtype)

        over(sz.rows // 64, one)

    def contract(left, weight, dst, count):
        def one(n):
            cols = tile(n, 256)
            dst[:, cols] = lax.dot_general(
                left[...], weight[cols, :], (((1,), (1,)), ((), ())), preferred_element_type=F32
            )

        over(count // 256, one)

    def backward(layer, unit):
        def freed(*which):
            if layer > 0:
                for name in which:
                    load(layer - 1, name)

        if layer < last:
            cast(gx, low)
            low_t[...] = low[...].T
            need(keys.gb)
            down_grad(layer, unit)
        freed(keys.gb)
        unit += 2
        need(keys.down_w, keys.p)

        def act_tile(n):
            cols = tile(n, 256)
            ga[:, :256] = lax.dot_general(
                low[...], r.down_w[cols, :], (((1,), (1,)), ((), ())), preferred_element_type=F32
            )

            def one(i):
                at = tile(i, 64)
                p = r.p[at, cols]
                slope = normal_below(p) + ROOT_TAU * p * jnp.exp(-0.5 * p * p)
                gp[at, cols] = (ga[at, :256] * slope).astype(BF16)

            over(sz.rows // 64, one)

        for quarter in range(4):
            over(sz.inner // 1024, lambda n: act_tile(n + quarter * (sz.inner // 1024)))
            units.passed(1.5)
        freed(keys.down_w, keys.p)
        need(keys.v)
        wide_t[...] = r.v[...].T
        freed(keys.v)
        for k in range(2):
            units.room(unit + k)

        def up_grad(b):
            value = jnp.dot(wide_t[...], gp[:, tile(b, 256)], preferred_element_type=F32)
            for s in range(4):
                for h in range(2):
                    at = place(h, s // 2, b % 2, (b // 2) % 2, b // 4)
                    for t in range(2):
                        held[(unit + t) % HELD, s % 2, h, at] = value[
                            s * 128 + h * 64 : s * 128 + h * 64 + 64, t * 128 : t * 128 + 128
                        ]

        over(8, up_grad)
        units.produced(unit, unit + 1)
        unit += 2
        units.passed(3)
        need(keys.up_w, keys.y1)
        contract(gp, r.up_w, grad, sz.width)
        freed(keys.up_w)
        units.passed(2)
        norm_back(r.y1, r.mlp_gain.at[layer : layer + 1], grad, gx, gy1, r.mlp_sum, sz.rows, 64)
        freed(keys.y1)
        cast(gy1, low)
        need(keys.states)

        def cast_state(i):
            hb[tile(i, sz.group), :] = r.states[tile(i + 1, sz.group), :].astype(BF16)

        if layer < last:
            over(sz.steps, cast_state)
        low_t[...] = low[...].T
        units.room(unit)
        units.passed(2)

        def out_grad(s):
            value = jnp.dot(low_t[...], hb[:, tile(s, 256)], preferred_element_type=F32)
            for b in range(8):
                for h in range(2):
                    at = place(h, s // 2, b % 2, (b // 2) % 2, b // 4)
                    held[unit % HELD, s % 2, h, at] = value[
                        b * 64 : b * 64 + 64, h * 128 : h * 128 + 128
                    ]

        over(4, out_grad)
        units.produced(unit)
        unit += 1
        units.passed(1.5)
        need(keys.out_w, keys.a, keys.b)
        contract(low, r.out_w, ga, sz.hidden)
        freed(keys.out_w)
        units.passed(1.5)
        for part in range(2):
            lanes = slice(part * half, (part + 1) * half)

            def totals(j, pair):
                at = tile(j, sz.group)
                mask = jnp.concatenate([keep[at, :]] * (half // LANES), axis=1)
                d = gate_weights(r.a[at, lanes], r.b[at, lanes])[0] * mask
                decay[at, lanes] = d
                return pair[0] * d, d * (ga[at, lanes] + pair[1])

            one = jnp.ones((sz.group, half), F32)
            pair = steps_of(sz.steps, 2, totals, (one, jnp.zeros_like(one)), reverse=True)
            r.chunk_p[:, lanes] = pair[0]
            r.chunk_t[:, lanes] = pair[1]
        scan_totals(r.chunk_p, r.chunk_t, sz, True, prefix, None, mine)
        flight = exchange_start(1, layer)
        units.passed(3)
        exchange_end(*flight, True)
        need(keys.zc)

        def gate_lanes(n):
            wide = 2 * LANES
            lanes = tile(n, wide)

            def walk(j, kept):
                m, bf, bi, bc = kept
                at = tile(j, sz.group)
                d = decay[at, lanes]
                q = ga[at, lanes] + m
                a, b, zc = r.a[at, lanes], r.b[at, lanes], r.zc[at, lanes]
                vm = jnp.concatenate([valid[at, :]] * 2, axis=1)
                km = jnp.concatenate([keep[at, :]] * 2, axis=1)
                fp, ip, inv = gate_weights(a, b)
                gf = q * (r.states[at, lanes] * km - zc * vm)
                parts = (
                    (gf * (a * inv) * fp).astype(BF16),
                    (-gf * (b * inv) * ip).astype(BF16),
                    (q * vm * ip).astype(BF16),
                )
                for part, value in enumerate(parts):
                    gz[at, pl.ds(pl.multiple_of(part * sz.hidden + n * wide, wide), wide)] = value
                return (d * q,) + tuple(
                    a + value.astype(F32) for a, value in zip((bf, bi, bc), parts)
                )

            zero = jnp.zeros((sz.group, wide), F32)
            _, *sums = steps_of(
                sz.steps, 4, walk, (enter[:, lanes], zero, zero, zero), reverse=True
            )
            for part, total in enumerate(sums):
                small[0, layer * 4 + part : layer * 4 + part + 1, lanes] = jnp.sum(
                    total, axis=0, keepdims=True
                )

        turns = sz.hidden // LANES // 4
        over(turns, gate_lanes)
        units.passed(2)
        over(turns, lambda n: gate_lanes(n + turns))
        freed(keys.a, keys.b, keys.zc, keys.states)
        units.passed(2)
        need(keys.u)
        wide_t[...] = r.u[...].T
        freed(keys.u)
        for k in range(2):
            units.room(unit + k)

        def gate_grad(b):
            cols = pl.ds(pl.multiple_of(b * 384, 128), 256)
            value = jnp.dot(wide_t[...], gz[:, cols], preferred_element_type=F32)
            for s in range(4):
                for h in range(2):
                    at = place(h, s // 2, b % 2, (b // 2) % 2, b // 4)
                    for t in range(2):
                        held[(unit + t) % HELD, s % 2, h, at] = value[
                            s * 128 + h * 64 : s * 128 + h * 64 + 64, t * 128 : t * 128 + 128
                        ]

        over(8, gate_grad)
        units.produced(unit, unit + 1)
        unit += 2
        units.passed(3)
        units.room(unit)

        def gate_rest(z):
            right = jnp.concatenate(
                [
                    gz[:, pl.ds(pl.multiple_of((2 * z + y) * 384 + 256, 128), 128)]
                    for y in range(2)
                ],
                axis=1,
            )
            value = jnp.dot(wide_t[...], right, preferred_element_type=F32)
            for s in range(4):
                for h in range(2):
                    for y in range(2):
                        at = place(h, s // 2, y, z % 2, z // 2)
                        held[unit % HELD, s % 2, h, at] = value[
                            s * 128 + h * 64 : s * 128 + h * 64 + 64, y * 128 : y * 128 + 128
                        ]

        over(4, gate_rest)
        units.produced(unit)
        unit += 1
        units.passed(1.5)
        need(keys.gate_w, keys.stream)
        contract(gz, r.gate_w, grad, sz.width)
        freed(keys.gate_w)
        units.passed(2.5)
        norm_back(r.stream, r.mix_gain.at[layer : layer + 1], grad, gy1, gx, r.mix_sum, sz.rows, 64)
        freed(keys.stream)
        row = slice(layer * 4 + 3, layer * 4 + 4)
        small[0, row, : sz.width] = jnp.sum(r.mix_sum[...], axis=0, keepdims=True)
        small[0, row, sz.width : 2 * sz.width] = jnp.sum(r.mlp_sum[...], axis=0, keepdims=True)
        units.passed(1.5)

    forward(0)
    keep_cotangent()
    for layer in range(1, layers):
        forward(layer)
    out_copies = from_steps(gy1, r.layer_out, r.out_sems)
    cast(low, gx)
    units.passed(2)
    for index, layer in enumerate(reversed(range(layers))):
        backward(layer, 8 * index)
    units.small_start()
    for copy in out_copies:
        copy.wait()
    out_copies = from_steps(gx, r.input_grad, r.out_sems)
    units.passed(1)
    units.drain()
    for copy in out_copies:
        copy.wait()
    total = small[STAGES]
    count = jnp.int32(0)
    for s in range(r.lens.shape[0]):
        for d in range(r.lens.shape[1]):
            count = count + r.lens[s, d]
    scale = 1.0 / (count.astype(F32) * sz.hidden)
    for layer in range(layers):
        for part in range(3):
            r.gate_bias_grad[layer : layer + 1, part * sz.hidden : (part + 1) * sz.hidden] = total[
                layer * 4 + part : layer * 4 + part + 1, : sz.hidden
            ]
        row = slice(layer * 4 + 3, layer * 4 + 4)
        r.mix_gain_grad[layer : layer + 1, :] = total[row, : sz.width]
        r.mlp_gain_grad[layer : layer + 1, :] = total[row, sz.width : 2 * sz.width]
        lanes = total[layer * 4 : layer * 4 + 1, sz.hidden : sz.hidden + LANES]
        r.forget_mean[layer : layer + 1, :] = (
            jnp.sum(lanes, axis=1, keepdims=True) * scale + jnp.zeros((1, LANES), F32)
        )


def run_whole_step(sz, layers, named):
    lengths = named["lengths"]
    rows, d, h, f = sz.rows, sz.width, sz.hidden, sz.inner
    vm = lambda *dims, kind=F32: pltpu.VMEM(dims, kind)
    sems = pltpu.SemaphoreType
    spec = dict(gate_bias=VMEM, mix_gain=VMEM, mlp_gain=VMEM)
    outputs = dict(
        layer_out=(shape(rows, d), ANY),
        input_grad=(shape(rows, d), ANY),
        gate_weight_grad=(shape(layers, 128, 384), VMEM),
        gate_bias_grad=(shape(layers, 3 * h), VMEM),
        out_weight_grad=(shape(layers, 64, 256), VMEM),
        up_weight_grad=(shape(layers, 128, 256), VMEM),
        down_weight_grad=(shape(layers, 64, 512), VMEM),
        mix_gain_grad=(shape(layers, d), VMEM),
        mlp_gain_grad=(shape(layers, d), VMEM),
        forget_mean=(shape(layers, LANES), VMEM),
    )
    results = len(outputs)
    kept = dict(
        u=((rows, d), BF16),
        a=((rows, h), F32),
        b=((rows, h), F32),
        zc=((rows, h), F32),
        states=((rows + sz.group, h), F32),
        y1=((rows, d), F32),
        v=((rows, d), BF16),
        p=((rows, f), F32),
        gb=((rows, f), BF16),
        stream=((rows, d), F32),
    )
    scratch = {}
    for name, (dims, kind) in kept.items():
        outputs[name + "_save"] = (shape(layers - 1, *dims, kind=kind), ANY)
        scratch[name] = vm(*dims, kind=kind)
    scratch.update(
        gate_w=vm(d, 3 * h, kind=BF16),
        out_w=vm(h, d, kind=BF16),
        up_w=vm(d, f, kind=BF16),
        down_w=vm(f, d, kind=BF16),
        valid=vm(rows, LANES),
        keep=vm(rows, LANES),
        gx=vm(rows, d),
        low=vm(rows, d, kind=BF16),
        low_t=vm(d, rows, kind=BF16),
        wide_t=vm(d, rows, kind=BF16),
        hb=vm(rows, h, kind=BF16),
        ga=vm(rows, h),
        gz=vm(rows, 3 * h, kind=BF16),
        grad=vm(rows, d),
        gy1=vm(rows, d),
        decay=vm(rows, h),
        chunk_p=vm(sz.group, h),
        chunk_t=vm(sz.group, h),
        prefix=vm(2, sz.group, h),
        enter=vm(sz.group, h),
        mine=vm(8, h),
        slots=vm(2, layers, sz.sections, 8, h),
        mlp_sum=vm(8, d),
        mix_sum=vm(8, d),
        held=vm(HELD, 2, 2, 16, BLOCK, LANES),
        small=vm(STAGES + 1, 8, SMALL),
        small_arrived=vm(STAGES, 8, SMALL),
        in_sems=sems.DMA((3,)),
        lens=pltpu.SMEM(lengths.shape, jnp.int32),
        out_sems=sems.DMA((d // LANES,)),
        natural=vm(d // LANES, rows, LANES),
        load_sems=sems.DMA((len(kept) + 4,)),
        save_sems=sems.DMA((len(kept) + 4,)),
        pair_send=sems.DMA((2, layers, sz.sections - 1)),
        pair_recv=sems.DMA((2, layers, sz.sections - 1)),
        send_sems=sems.DMA((SENDS, 2 * STAGES - 1)),
        recv_sems=sems.DMA((max(RINGS), 2 * STAGES - 1)),
        credits=sems.REGULAR((2 * STAGES - 1,)),
        small_send=sems.DMA((STAGES,)),
        small_recv=sems.DMA((STAGES,)),
    )
    for stage in range(STAGES):
        scratch[f"arrived{stage}"] = vm(RINGS[stage], 2, 16 >> stage, BLOCK, LANES)
    names = list(named) + list(outputs) + list(scratch)
    out = pl.pallas_call(
        functools.partial(whole_step, sz, layers, names),
        out_shape=tuple(value for value, _ in outputs.values()),
        in_specs=[spec.get(name, ANY) for name in named],
        out_specs=[place_of for _, place_of in outputs.values()],
        scratch_shapes=list(scratch.values()),
        compiler_params=pltpu.CompilerParams(
            collective_id=4, has_side_effects=True, vmem_limit_bytes=LIMIT
        ),
        name="whole_step",
    )(*named.values())
    return out[:results]


def deliver_kernel(count, *refs):
    sources, targets, held = refs[:count], refs[count : 2 * count], refs[2 * count : 3 * count - 1]
    sems = refs[3 * count - 1]
    arrivals = [
        pltpu.make_async_copy(sources[i], held[i], sems.at[0, i]) for i in range(count - 1)
    ]
    departures = [
        pltpu.make_async_copy(held[i], targets[i], sems.at[1, i]) for i in range(count - 1)
    ]
    for copy in arrivals:
        copy.start()
    for layer in range(targets[-1].shape[0]):
        targets[-1][layer] = sources[-1][layer, 0]
    for arrival, departure in zip(arrivals, departures):
        arrival.wait()
        departure.start()
    for copy in departures:
        copy.wait()


def deliver(values):
    count = len(values)
    scalars = pl.BlockSpec(memory_space=pltpu.SMEM)
    shapes = [shape(*value.shape) for value in values[:-1]] + [shape(values[-1].shape[0])]
    return pl.pallas_call(
        functools.partial(deliver_kernel, count),
        out_shape=tuple(shapes),
        in_specs=[ANY] * (count - 1) + [scalars],
        out_specs=[ANY] * (count - 1) + [scalars],
        scratch_shapes=[pltpu.VMEM(value.shape, F32) for value in values[:-1]]
        + [pltpu.SemaphoreType.DMA((2, count - 1))],
        compiler_params=pltpu.CompilerParams(vmem_limit_bytes=LIMIT),
        name="deliver",
    )(*values)


def mask_kernel(sizes, lens, valid, keep):
    fill_masks(lens, valid, keep, sizes)


def body(
    activations,
    cotangent,
    lengths,
    gate_weight,
    gate_bias,
    out_weight,
    up_weight,
    down_weight,
    mix_gain,
    mlp_gain,
):
    micro, span, width = activations.shape
    layers = gate_weight.shape[0]
    sz = Sizes(
        micro, span, width, out_weight.shape[1], up_weight.shape[2], lax.axis_size("section")
    )

    blocks = (width // 4, 3 * sz.hidden // 8, width // 8, sz.inner // 4, sz.hidden // 4)
    axes = (lax.axis_size("section"), lax.axis_size("batch"))
    if axes == (4, 8) and blocks == (128, 384, 64, 512, 256):
        out = run_whole_step(
            sz,
            layers,
            dict(
                activations=activations.reshape(sz.rows, width),
                cotangent=cotangent.reshape(sz.rows, width),
                lengths=lengths.T,
                gate_bias=gate_bias,
                mix_gain=mix_gain,
                mlp_gain=mlp_gain,
                gate_hbm=gate_weight,
                out_hbm=out_weight,
                up_hbm=up_weight,
                down_hbm=down_weight,
            ),
        )
        stream_out, input_grad, gate_g, bias_g, out_g, up_g, down_g, *rest = deliver(out)
        return (
            stream_out.reshape(activations.shape),
            input_grad.reshape(activations.shape),
            gate_g,
            bias_g,
            out_g.transpose(0, 2, 1),
            up_g,
            down_g.transpose(0, 2, 1),
            *rest,
        )

    def arranged(value):
        value = value.astype(F32).reshape(micro, CHUNKS, sz.steps, width)
        return value.transpose(2, 0, 1, 3).reshape(sz.rows, width)

    def restored(value):
        value = value.reshape(sz.steps, micro, CHUNKS, width).transpose(1, 2, 0, 3)
        return value.reshape(micro, span, width)

    masks = pl.pallas_call(
        functools.partial(mask_kernel, sz),
        out_shape=(shape(sz.rows, LANES), shape(sz.rows, LANES)),
        in_specs=[pl.BlockSpec(memory_space=pltpu.SMEM)],
        out_specs=[VMEM] * 2,
        name="masks",
    )(lengths)
    weights = (gate_weight, out_weight, up_weight, down_weight)
    stream = arranged(activations)
    streams, saved, forgets = [], [], []
    for layer in range(layers):
        streams.append(stream)
        stream, *kept, forget, pairs = run_forward(
            sz,
            layer,
            stream,
            masks,
            gate_bias[layer : layer + 1],
            mix_gain[layer : layer + 1],
            mlp_gain[layer : layer + 1],
            weights,
        )
        saved.append((*kept, pairs))
        forgets.append(forget)
    layer_out = restored(stream)
    gx = arranged(cotangent)
    true_count = jnp.sum(lengths).astype(F32)
    forgets = [jnp.sum(forget) for forget in forgets]
    sums, small = [None] * layers, [None] * layers
    for layer in reversed(range(layers)):
        gx, gate_g, out_g, up_g, down_g, bias_g, mix_g, mlp_g = run_backward(
            sz,
            layer,
            gx,
            streams[layer],
            masks,
            mix_gain[layer : layer + 1],
            mlp_gain[layer : layer + 1],
            saved[layer],
            weights,
        )
        sums[layer] = (gate_g, out_g.T, up_g, down_g.T)
        small[layer] = tuple(jnp.sum(part, axis=0) for part in (bias_g, mix_g, mlp_g))
    input_grad = restored(gx)
    stacked = tuple(jnp.stack(parts) for parts in zip(*sums))
    partial_sums = lax.psum_scatter(stacked, "section", scatter_dimension=1, tiled=True)
    large = lax.psum_scatter(partial_sums, "batch", scatter_dimension=2, tiled=True)
    bias_grad, mix_grad, mlp_grad = (jnp.stack(parts) for parts in zip(*small))
    bias_grad, mix_grad, mlp_grad, forget = lax.psum(
        (bias_grad, mix_grad, mlp_grad, jnp.stack(forgets)), ("section", "batch")
    )
    forget_mean = forget / (true_count * sz.hidden)
    return (
        layer_out,
        input_grad,
        large[0],
        bias_grad,
        large[1],
        large[2],
        large[3],
        mix_grad,
        mlp_grad,
        forget_mean,
    )


def solution(mesh):
    stream = P("batch", "section", None)
    block = P(None, "section", "batch")
    return jax.shard_map(
        body,
        mesh=mesh,
        in_specs=(stream, stream) + (P(),) * 8,
        out_specs=(stream, stream, block, P(), block, block, block, P(), P(), P()),
        check_vma=False,
    )
```

profile of v0, /device:TPU:0, one launch (start us, length us, event | category | flops | bytes accessed | tf_op | source)
XLA Modules:
  0.0 206.2 jit_solution(2845420588048433788)
XLA Ops:
  0.6 201.2 %whole_step.1 = (f32[512,512]{1,0:T(8,128)}, f32[512,512]{1,0:T(8,128)}, f32[2,128,384]{2,1,0:T(8,128)}, f32[2,3072]{1,0:T(2,128)}, f32[2,64,256]{2,1,0:T(8,128)...) custom-call(bf16[512,512]{1,0:T(8,128)(2,1)} %bitcast.7, ...), custom_call_target="tpu_custom_call" | custom-call | tf_op jit(solution)/shard_map/whole_step/pallas_call | solution.py:1513
  201.8 4.3 %deliver.1 = (f32[512,512]{1,0:T(8,128)}, f32[512,512]{1,0:T(8,128)}, f32[2,128,384]{2,1,0:T(8,128)}, f32[2,3072]{1,0:T(2,128)}, f32[2,64,256]{2,1,0:T(8,128)}, ...) custom-call(f32[512,512]{1,0:T(8,128)} %get-tuple-element.30.refs_0_, ...), custom_call_target="tpu_custom_call" | custom-call | tf_op jit(solution)/shard_map/deliver/pallas_call | solution.py:1551
where the time goes:
time: 207 us; the launch traced here: 206 us
  Pallas kernels  205 us (99%)
    pallas_call x1, Pallas kernels, run_whole_step(): pl.pallas_call(functools.partial(whole_step, sz, layers, names), out_shap...  201 us
    pallas_call x1, Pallas kernels, deliver(): pl.pallas_call(functools.partial(deliver_kernel, count), out_shape=tuple(...  4.26 us

commit v1 on v0

--- a/solution.py
+++ b/solution.py
@@ -160,6 +160,35 @@
             a = jnp.where(reached, pk * a + tk, a)
         at = slice(s * 8, s * 8 + 8)
         enter[at, :] = prefix[0, at, :] * a + prefix[1, at, :]
+
+
+def part_totals(first, second, sizes, reverse, prefix, mine, lanes):
+    for s in range(sizes.micro):
+        p = jnp.ones((1, lanes.stop - lanes.start), F32)
+        t = jnp.zeros_like(p)
+        for c in reversed(range(CHUNKS)) if reverse else range(CHUNKS):
+            at = s * 8 + c
+            prefix[0, at : at + 1, lanes] = p
+            prefix[1, at : at + 1, lanes] = t
+            pc = first[at : at + 1, lanes]
+            t = pc * t + second[at : at + 1, lanes]
+            p = p * pc
+        mine[s : s + 1, lanes] = p
+        mine[sizes.micro + s : sizes.micro + s + 1, lanes] = t
+
+
+def part_enter(slots, prefix, enter, sizes, reverse, lanes):
+    me = lax.axis_index("section")
+    for s in range(sizes.micro):
+        a = jnp.zeros((1, lanes.stop - lanes.start), F32)
+        order = range(sizes.sections - 1, 0, -1) if reverse else range(sizes.sections - 1)
+        for k in order:
+            reached = k > me if reverse else k < me
+            pk = slots[k, s : s + 1, lanes]
+            tk = slots[k, sizes.micro + s : sizes.micro + s + 1, lanes]
+            a = jnp.where(reached, pk * a + tk, a)
+        at = slice(s * 8, s * 8 + 8)
+        enter[at, lanes] = prefix[0, at, lanes] * a + prefix[1, at, lanes]
 
 
 class Sizes:
@@ -642,8 +671,8 @@
 
 BLOCK = 64
 HELD = 3
-RINGS = (4, 5, 5, 5, 5)
-SENDS = 8
+RINGS = (4, 5, 6, 16, 16)
+SENDS = 16
 STAGES = 5
 WINDOW = 4
 SMALL = 1280
@@ -902,6 +931,7 @@
     natural = r.natural
     last = layers - 1
     half = sz.hidden // 2
+    z0, z1 = ga.at[:, :768], r.z1
     drive = r.p.at[:, : sz.hidden]
     homes = dict(gate_w=r.gate_hbm, out_w=r.out_hbm, up_w=r.up_hbm, down_w=r.down_hbm)
     homes.update(u=r.u_save, a=r.a_save, b=r.b_save, zc=r.zc_save, states=r.states_save)
@@ -996,30 +1026,47 @@
 
     to_steps(hb.at[:, : sz.width], put_gx)
 
-    def exchange_start(way, layer):
+    parts = [slice(part * half, (part + 1) * half) for part in range(2)]
+
+    def exchange_start(way, layer, part):
+        lanes = parts[part]
         slots = r.slots.at[way, layer]
         me = lax.axis_index("section")
         copies = []
         for hop in range(1, sz.sections):
             copies.append(
                 pltpu.make_async_remote_copy(
-                    src_ref=mine,
-                    dst_ref=slots.at[me],
-                    send_sem=r.pair_send.at[way, layer, hop - 1],
-                    recv_sem=r.pair_recv.at[way, layer, hop - 1],
+                    src_ref=mine.at[:, lanes],
+                    dst_ref=slots.at[me, :, lanes],
+                    send_sem=r.pair_send.at[way, layer, part, hop - 1],
+                    recv_sem=r.pair_recv.at[way, layer, part, hop - 1],
                     device_id={"section": lax.rem(me + hop, sz.sections)},
                     device_id_type=MESH,
                 )
             )
         for copy in copies:
             copy.start()
-        slots[me] = mine[...]
+        slots[me, :, lanes] = mine[:, lanes]
         return slots, copies
 
-    def exchange_end(slots, copies, reverse):
+    def exchange_end(slots, copies, reverse, part):
         for copy in copies:
             copy.wait()
-        scan_enter(slots, prefix, enter, sz, reverse)
+        part_enter(slots, prefix, enter, sz, reverse, parts[part])
+
+    def in_turn(count, dots, rest, after=None):
+        zs = (z0, z1)
+        over(sz.rows // 256, lambda i: dots(0, zs[0], i))
+        for n in range(count):
+
+            def both(i):
+                if n + 1 < count:
+                    dots(n + 1, zs[(n + 1) % 2], i)
+                rest(n, zs[n % 2], i)
+
+            over(sz.rows // 256, both)
+            if after is not None:
+                after(n)
 
     def keep_cotangent():
         cot_load.wait()
@@ -1033,7 +1080,7 @@
     def forward(layer):
         stream = r.stream if layer > 0 else gx
         settled(keys.u)
-        norm_rows(stream, r.mix_gain.at[layer : layer + 1], r.u, sz.rows, 64)
+        norm_rows(stream, r.mix_gain.at[layer : layer + 1], r.u, sz.rows, 128)
         save(layer, keys.u)
         if layer == 0:
             save(layer, keys.stream, gx)
@@ -1042,63 +1089,68 @@
         hw = 256
         bias = r.gate_bias
 
-        def gate_tile(n, forget):
+        def gate_dots(n, z, i):
+            rows = tile(i, 256)
             for part in range(3):
-                cols = pl.ds(pl.multiple_of(part * sz.hidden + n * hw, hw), hw)
-                ga[:, part * hw : (part + 1) * hw] = (
-                    jnp.dot(r.u[...], r.gate_w[:, cols], preferred_element_type=F32)
+                cols = slice(part * sz.hidden + n * hw, part * sz.hidden + (n + 1) * hw)
+                z[rows, part * hw : (part + 1) * hw] = (
+                    jnp.dot(r.u[rows, :], r.gate_w[:, cols], preferred_element_type=F32)
                     + bias[layer : layer + 1, cols]
                 )
-            return lax.fori_loop(0, sz.rows // 64, functools.partial(gate_rows, n), forget)
-
-        def gate_rows(n, i, forget):
-            at = tile(i, 64)
-            vm, km = valid[at, :], keep[at, :]
-            for lane in range(hw // LANES):
-                zf, zi, zc = (
-                    ga[at, part * hw + lane * LANES : part * hw + (lane + 1) * LANES]
-                    for part in range(3)
-                )
-                dst = pl.ds(pl.multiple_of(n * hw + lane * LANES, LANES), LANES)
-                a = jnp.exp(jnp.minimum(-zf, 86.0))
-                b = jnp.exp(jnp.minimum(-zi, 86.0))
-                fp, ip, _ = gate_weights(a, b)
-                decay[at, dst] = fp * km
-                drive[at, dst] = ip * zc * vm
-                r.a[at, dst] = a
-                r.b[at, dst] = b
-                r.zc[at, dst] = zc
-                forget = forget + jnp.sum((fp * vm).reshape(8, 8, LANES), axis=0)
-            return forget
-
-        forget = lax.fori_loop(0, sz.hidden // hw, gate_tile, jnp.zeros((8, LANES), F32))
+
+        def gate_rest(n, z, i):
+            for chunk in range(4):
+                at = pl.ds(pl.multiple_of(i * 256 + chunk * 64, 64), 64)
+                vm, km = valid[at, :], keep[at, :]
+                for lane in range(hw // LANES):
+                    zf, zi, zc = (
+                        z[at, part * hw + lane * LANES : part * hw + (lane + 1) * LANES]
+                        for part in range(3)
+                    )
+                    dst = slice(n * hw + lane * LANES, n * hw + (lane + 1) * LANES)
+                    a = jnp.exp(jnp.minimum(-zf, 86.0))
+                    b = jnp.exp(jnp.minimum(-zi, 86.0))
+                    fp, ip, _ = gate_weights(a, b)
+                    decay[at, dst] = fp * km
+                    drive[at, dst] = ip * zc * vm
+                    r.a[at, dst] = a
+                    r.b[at, dst] = b
+                    r.zc[at, dst] = zc
+                    r.forget[...] += jnp.sum((fp * vm).reshape(8, 8, LANES), axis=0)
+
+        flights = []
+
+        def gate_after(n):
+            if n % 2 == 0:
+                return
+            lanes = parts[n // 2]
+
+            def totals(j, pair):
+                at = tile(j, sz.group)
+                d = decay[at, lanes]
+                return pair[0] * d, pair[1] * d + drive[at, lanes]
+
+            one = jnp.ones((sz.group, half), F32)
+            pair = steps_of(sz.steps, 2, totals, (one, jnp.zeros_like(one)))
+            r.chunk_p[:, lanes] = pair[0]
+            r.chunk_t[:, lanes] = pair[1]
+            part_totals(r.chunk_p, r.chunk_t, sz, False, prefix, mine, lanes)
+            flights.append(exchange_start(0, layer, n // 2))
+
+        r.forget[...] = jnp.zeros_like(r.forget)
+        in_turn(sz.hidden // hw, gate_dots, gate_rest, gate_after)
         small[0, layer * 4 : layer * 4 + 1, sz.hidden : sz.hidden + LANES] = jnp.sum(
-            forget, axis=0, keepdims=True
+            r.forget[...], axis=0, keepdims=True
         )
         for name in (keys.a, keys.b, keys.zc):
             save(layer, name)
         if layer < last:
             load(layer + 1, keys.gate_w)
-        for part in range(2):
-            lanes = slice(part * half, (part + 1) * half)
-
-            def totals(j, pair):
-                at = tile(j, sz.group)
-                d = decay[at, lanes]
-                return pair[0] * d, pair[1] * d + drive[at, lanes]
-
-            one = jnp.ones((sz.group, half), F32)
-            pair = steps_of(sz.steps, 2, totals, (one, jnp.zeros_like(one)))
-            r.chunk_p[:, lanes] = pair[0]
-            r.chunk_t[:, lanes] = pair[1]
-        scan_totals(r.chunk_p, r.chunk_t, sz, False, prefix, None, mine)
-        flight = exchange_start(0, layer)
         settled(keys.states, keys.y1, keys.v, keys.gb, keys.stream)
-        exchange_end(*flight, False)
         states = r.states
-        states[0 : sz.group, :] = enter[...]
-        for part in range(2):
-            lanes = slice(part * half, (part + 1) * half)
+        for part, lanes in enumerate(parts):
+            exchange_end(*flights[part], False, part)
+            states[0 : sz.group, lanes] = enter[:, lanes]
 
             def walk(j, h):
                 at = tile(j, sz.group)
@@ -1121,22 +1173,25 @@
         save(layer, keys.y1)
         if layer < last:
             load(layer + 1, keys.out_w)
-        norm_rows(r.y1, r.mlp_gain.at[layer : layer + 1], r.v, sz.rows, 64)
+        norm_rows(r.y1, r.mlp_gain.at[layer : layer + 1], r.v, sz.rows, 128)
         save(layer, keys.v)
         need(keys.up_w)
 
-        def up_tile(n):
-            cols = tile(n, 256)
-            r.p[:, cols] = jnp.dot(r.v[...], r.up_w[:, cols], preferred_element_type=F32)
-
-            def one(i):
-                at = tile(i, 64)
-                p = r.p[at, cols]
+        def up_dots(n, z, i):
+            rows = tile(i, 256)
+            z[rows, :256] = jnp.dot(
+                r.v[rows, :], r.up_w[:, n * 256 : (n + 1) * 256], preferred_element_type=F32
+            )
+
+        def up_rest(n, z, i):
+            cols = slice(n * 256, (n + 1) * 256)
+            for chunk in range(4):
+                at = pl.ds(pl.multiple_of(i * 256 + chunk * 64, 64), 64)
+                p = z[at, :256]
+                r.p[at, cols] = p
                 r.gb[at, cols] = (p * normal_below(p)).astype(BF16)
 
-            over(sz.rows // 64, one)
-
-        over(sz.inner // 256, up_tile)
+        in_turn(sz.inner // 256, up_dots, up_rest)
         save(layer, keys.p)
         save(layer, keys.gb)
         if layer < last:
@@ -1205,23 +1260,24 @@
         unit += 2
         need(keys.down_w, keys.p)
 
-        def act_tile(n):
-            cols = tile(n, 256)
-            ga[:, :256] = lax.dot_general(
-                low[...], r.down_w[cols, :], (((1,), (1,)), ((), ())), preferred_element_type=F32
+        def act_dots(n, z, i):
+            rows = tile(i, 256)
+            z[rows, :256] = lax.dot_general(
+                low[rows, :],
+                r.down_w[n * 256 : (n + 1) * 256, :],
+                (((1,), (1,)), ((), ())),
+                preferred_element_type=F32,
             )
 
-            def one(i):
-                at = tile(i, 64)
+        def act_rest(n, z, i):
+            cols = slice(n * 256, (n + 1) * 256)
+            for chunk in range(4):
+                at = pl.ds(pl.multiple_of(i * 256 + chunk * 64, 64), 64)
                 p = r.p[at, cols]
                 slope = normal_below(p) + ROOT_TAU * p * jnp.exp(-0.5 * p * p)
-                gp[at, cols] = (ga[at, :256] * slope).astype(BF16)
-
-            over(sz.rows // 64, one)
-
-        for quarter in range(4):
-            over(sz.inner // 1024, lambda n: act_tile(n + quarter * (sz.inner // 1024)))
-            units.passed(1.5)
+                gp[at, cols] = (z[at, :256] * slope).astype(BF16)
+
+        in_turn(sz.inner // 256, act_dots, act_rest, lambda n: units.passed(0.6))
         freed(keys.down_w, keys.p)
         need(keys.v)
         wide_t[...] = r.v[...].T
@@ -1278,24 +1334,26 @@
         contract(low, r.out_w, ga, sz.hidden)
         freed(keys.out_w)
         units.passed(1.5)
-        for part in range(2):
-            lanes = slice(part * half, (part + 1) * half)
+        flights = []
+        for part, lanes in enumerate(parts):
 
             def totals(j, pair):
                 at = tile(j, sz.group)
-                mask = jnp.concatenate([keep[at, :]] * (half // LANES), axis=1)
-                d = gate_weights(r.a[at, lanes], r.b[at, lanes])[0] * mask
-                decay[at, lanes] = d
+                if layer < last:
+                    mask = jnp.concatenate([keep[at, :]] * (half // LANES), axis=1)
+                    d = gate_weights(r.a[at, lanes], r.b[at, lanes])[0] * mask
+                    decay[at, lanes] = d
+                else:
+                    d = decay[at, lanes]
                 return pair[0] * d, d * (ga[at, lanes] + pair[1])
 
             one = jnp.ones((sz.group, half), F32)
             pair = steps_of(sz.steps, 2, totals, (one, jnp.zeros_like(one)), reverse=True)
             r.chunk_p[:, lanes] = pair[0]
             r.chunk_t[:, lanes] = pair[1]
-        scan_totals(r.chunk_p, r.chunk_t, sz, True, prefix, None, mine)
-        flight = exchange_start(1, layer)
-        units.passed(3)
-        exchange_end(*flight, True)
+            part_totals(r.chunk_p, r.chunk_t, sz, True, prefix, mine, lanes)
+            flights.append(exchange_start(1, layer, part))
+            units.passed(1.5)
         need(keys.zc)
 
         def gate_lanes(n):
@@ -1333,11 +1391,11 @@
                 )
 
         turns = sz.hidden // LANES // 4
-        over(turns, gate_lanes)
-        units.passed(2)
-        over(turns, lambda n: gate_lanes(n + turns))
+        for part in range(2):
+            exchange_end(*flights[part], True, part)
+            over(turns, lambda n: gate_lanes(n + part * turns))
+            units.passed(2)
         freed(keys.a, keys.b, keys.zc, keys.states)
-        units.passed(2)
         need(keys.u)
         wide_t[...] = r.u[...].T
         freed(keys.u)
@@ -1477,6 +1535,8 @@
         low_t=vm(d, rows, kind=BF16),
         wide_t=vm(d, rows, kind=BF16),
         hb=vm(rows, h, kind=BF16),
+        z1=vm(rows, 768),
+        forget=vm(8, LANES),
         ga=vm(rows, h),
         gz=vm(rows, 3 * h, kind=BF16),
         grad=vm(rows, d),
@@ -1499,8 +1559,8 @@
         natural=vm(d // LANES, rows, LANES),
         load_sems=sems.DMA((len(kept) + 4,)),
         save_sems=sems.DMA((len(kept) + 4,)),
-        pair_send=sems.DMA((2, layers, sz.sections - 1)),
-        pair_recv=sems.DMA((2, layers, sz.sections - 1)),
+        pair_send=sems.DMA((2, layers, 2, sz.sections - 1)),
+        pair_recv=sems.DMA((2, layers, 2, sz.sections - 1)),
         send_sems=sems.DMA((SENDS, 2 * STAGES - 1)),
         recv_sems=sems.DMA((max(RINGS), 2 * STAGES - 1)),
         credits=sems.REGULAR((2 * STAGES - 1,)),

time: 207 us -> 200 us (0.966)
  Pallas kernels: 205 us -> 199 us
    pallas_call x1, Pallas kernels: 201 us -> 195 us  [run_whole_step(): pl.pallas_call(functools.partial(whole_step, sz, layers, names), out_shap...]
where the time goes in v1:
time: 200 us
  Pallas kernels  199 us (100%)
    pallas_call x1, Pallas kernels, run_whole_step(): pl.pallas_call(functools.partial(whole_step, sz, layers, names), out_shap...  195 us
    pallas_call x1, Pallas kernels, deliver(): pl.pallas_call(functools.partial(deliver_kernel, count), out_shape=tuple(...  4.26 us

profile of v1, /device:TPU:0, one launch (start us, length us, event | category | flops | bytes accessed | tf_op | source)
XLA Modules:
  0.0 200.1 jit_solution(14367464571628998854)
XLA Ops:
  0.6 195.1 %whole_step.1 = (f32[512,512]{1,0:T(8,128)}, f32[512,512]{1,0:T(8,128)}, f32[2,128,384]{2,1,0:T(8,128)}, f32[2,3072]{1,0:T(2,128)}, f32[2,64,256]{2,1,0:T(8,128)...) custom-call(bf16[512,512]{1,0:T(8,128)(2,1)} %bitcast.7, ...), custom_call_target="tpu_custom_call" | custom-call | tf_op jit(solution)/shard_map/whole_step/pallas_call | solution.py:1573
  195.7 4.3 %deliver.1 = (f32[512,512]{1,0:T(8,128)}, f32[512,512]{1,0:T(8,128)}, f32[2,128,384]{2,1,0:T(8,128)}, f32[2,3072]{1,0:T(2,128)}, f32[2,64,256]{2,1,0:T(8,128)}, ...) custom-call(f32[512,512]{1,0:T(8,128)} %get-tuple-element.30.refs_0_, ...), custom_call_target="tpu_custom_call" | custom-call | tf_op jit(solution)/shard_map/deliver/pallas_call | solution.py:1611

commit v2 on v1

--- a/solution.py
+++ b/solution.py
@@ -700,6 +700,7 @@
         self.links = ("core", "x", "y", "z")
         self.free_at = dict.fromkeys(self.links, 0.0)
         self.flying = dict.fromkeys(self.links, 0)
+        self.window = dict.fromkeys(self.links, WINDOW)
         self.queues = {link: [] for link in self.links}
         self.ready = {}
         self.summed = set()
@@ -762,7 +763,7 @@
 
     def pump(self):
         for link, queue in self.queues.items():
-            while self.flying[link] < WINDOW:
+            while self.flying[link] < self.window[link]:
                 key = next((key for key in queue if self.has_place(*key)), None)
                 if key is None:
                     break
@@ -774,18 +775,27 @@
                     pl.semaphore_wait(self.credits.at[at], 1)
                 self.copies[key] = self.copy(*key)
                 self.copies[key].start()
-                size = (32 if stage == 0 else 16 >> stage) * BLOCK * LANES * 4
-                rate = 250e3 if link == "core" else 45e3
-                self.free_at[link] = max(self.now, self.free_at[link]) + size / rate
-                self.ready[key] = self.free_at[link] + 1.5
+                blocks = 32 if stage == 0 else 16 >> stage
+                self.ready[key] = self.expect(link, blocks * BLOCK * LANES * 4)
+
+    def expect(self, link, size):
+        rate = 250e3 if link == "core" else 45e3
+        self.free_at[link] = max(self.now, self.free_at[link]) + size / rate
+        return self.free_at[link] + 1.5
+
+    def hold(self, link, window):
+        self.window[link] = window
+        self.pump()
 
     def push(self, unit, stage, half):
         self.queues[self.link(stage, half)].append((unit, stage, half))
         self.pump()
 
-    def produced(self, *which):
+    def produced(self, us, *which):
+        self.now += us
         for unit in which:
             self.push(unit, 0, 0)
+        self.passed(0)
 
     def add(self, dst, src, count):
         turn = min(count, 4)
@@ -1226,8 +1236,7 @@
                     ]
 
         over(8, one)
-        units.produced(unit, unit + 1)
-        units.passed(3)
+        units.produced(2, unit, unit + 1)
 
     def cast(src, dst):
         def one(i):
@@ -1245,19 +1254,60 @@
 
         over(count // 256, one)
 
+    def up_grad(layer, unit):
+        need(keys.v)
+        wide_t[...] = r.v[...].T
+        for k in range(2):
+            units.room(unit + k)
+
+        def one(b):
+            value = jnp.dot(wide_t[...], gp[:, tile(b, 256)], preferred_element_type=F32)
+            for s in range(4):
+                for h in range(2):
+                    at = place(h, s // 2, b % 2, (b // 2) % 2, b // 4)
+                    for t in range(2):
+                        held[(unit + t) % HELD, s % 2, h, at] = value[
+                            s * 128 + h * 64 : s * 128 + h * 64 + 64, t * 128 : t * 128 + 128
+                        ]
+
+        over(8, one)
+        units.produced(2.5, unit, unit + 1)
+
+    def out_grad(layer, unit):
+        def cast_state(i):
+            hb[tile(i, sz.group), :] = r.states[tile(i + 1, sz.group), :].astype(BF16)
+
+        if layer < last:
+            over(sz.steps, cast_state)
+        low_t[...] = low[...].T
+        units.room(unit)
+
+        def one(s):
+            value = jnp.dot(low_t[...], hb[:, tile(s, 256)], preferred_element_type=F32)
+            for b in range(8):
+                for h in range(2):
+                    at = place(h, s // 2, b % 2, (b // 2) % 2, b // 4)
+                    held[unit % HELD, s % 2, h, at] = value[
+                        b * 64 : b * 64 + 64, h * 128 : h * 128 + 128
+                    ]
+
+        over(4, one)
+        units.produced(1.2, unit)
+
     def backward(layer, unit):
+        late = layer < last
+
         def freed(*which):
             if layer > 0:
                 for name in which:
                     load(layer - 1, name)
 
-        if layer < last:
+        if late:
             cast(gx, low)
             low_t[...] = low[...].T
-            need(keys.gb)
-            down_grad(layer, unit)
-        freed(keys.gb)
-        unit += 2
+            units.passed(1)
+        else:
+            freed(keys.gb)
         need(keys.down_w, keys.p)
 
         def act_dots(n, z, i):
@@ -1279,61 +1329,25 @@
 
         in_turn(sz.inner // 256, act_dots, act_rest, lambda n: units.passed(0.6))
         freed(keys.down_w, keys.p)
-        need(keys.v)
-        wide_t[...] = r.v[...].T
-        freed(keys.v)
-        for k in range(2):
-            units.room(unit + k)
-
-        def up_grad(b):
-            value = jnp.dot(wide_t[...], gp[:, tile(b, 256)], preferred_element_type=F32)
-            for s in range(4):
-                for h in range(2):
-                    at = place(h, s // 2, b % 2, (b // 2) % 2, b // 4)
-                    for t in range(2):
-                        held[(unit + t) % HELD, s % 2, h, at] = value[
-                            s * 128 + h * 64 : s * 128 + h * 64 + 64, t * 128 : t * 128 + 128
-                        ]
-
-        over(8, up_grad)
-        units.produced(unit, unit + 1)
-        unit += 2
-        units.passed(3)
+        if not late:
+            up_grad(layer, unit + 2)
+            freed(keys.v)
         need(keys.up_w, keys.y1)
         contract(gp, r.up_w, grad, sz.width)
         freed(keys.up_w)
-        units.passed(2)
+        units.passed(1.5)
         norm_back(r.y1, r.mlp_gain.at[layer : layer + 1], grad, gx, gy1, r.mlp_sum, sz.rows, 64)
         freed(keys.y1)
         cast(gy1, low)
         need(keys.states)
-
-        def cast_state(i):
-            hb[tile(i, sz.group), :] = r.states[tile(i + 1, sz.group), :].astype(BF16)
-
-        if layer < last:
-            over(sz.steps, cast_state)
-        low_t[...] = low[...].T
-        units.room(unit)
         units.passed(2)
-
-        def out_grad(s):
-            value = jnp.dot(low_t[...], hb[:, tile(s, 256)], preferred_element_type=F32)
-            for b in range(8):
-                for h in range(2):
-                    at = place(h, s // 2, b % 2, (b // 2) % 2, b // 4)
-                    held[unit % HELD, s % 2, h, at] = value[
-                        b * 64 : b * 64 + 64, h * 128 : h * 128 + 128
-                    ]
-
-        over(4, out_grad)
-        units.produced(unit)
-        unit += 1
-        units.passed(1.5)
+        units.hold("x", 1)
+        if not late:
+            out_grad(layer, unit + 4)
         need(keys.out_w, keys.a, keys.b)
         contract(low, r.out_w, ga, sz.hidden)
         freed(keys.out_w)
-        units.passed(1.5)
+        units.passed(1)
         flights = []
         for part, lanes in enumerate(parts):
 
@@ -1353,8 +1367,18 @@
             r.chunk_t[:, lanes] = pair[1]
             part_totals(r.chunk_p, r.chunk_t, sz, True, prefix, mine, lanes)
             flights.append(exchange_start(1, layer, part))
-            units.passed(1.5)
+            carried = [units.expect(link, 16384) for link in ("core", "x", "x")]
+            if part:
+                units.hold("x", WINDOW)
+            units.passed(0.8)
         need(keys.zc)
+        if late:
+            need(keys.gb)
+            down_grad(layer, unit)
+            up_grad(layer, unit + 2)
+            out_grad(layer, unit + 4)
+        unit += 5
+        units.now = max(units.now, *carried)
 
         def gate_lanes(n):
             wide = 2 * LANES
@@ -1394,7 +1418,7 @@
         for part in range(2):
             exchange_end(*flights[part], True, part)
             over(turns, lambda n: gate_lanes(n + part * turns))
-            units.passed(2)
+            units.passed(1.8)
         freed(keys.a, keys.b, keys.zc, keys.states)
         need(keys.u)
         wide_t[...] = r.u[...].T
@@ -1414,9 +1438,8 @@
                         ]
 
         over(8, gate_grad)
-        units.produced(unit, unit + 1)
+        units.produced(3, unit, unit + 1)
         unit += 2
-        units.passed(3)
         units.room(unit)
 
         def gate_rest(z):
@@ -1437,9 +1460,8 @@
                         ]
 
         over(4, gate_rest)
-        units.produced(unit)
+        units.produced(1.5, unit)
         unit += 1
-        units.passed(1.5)
         need(keys.gate_w, keys.stream)
         contract(gz, r.gate_w, grad, sz.width)
         freed(keys.gate_w)

time: 200 us -> 200 us (level)
  no operation moved by 1% of the time
where the time goes in v2:
time: 200 us; the launch traced here: 199 us
  Pallas kernels  199 us (100%)
    pallas_call x1, Pallas kernels, run_whole_step(): pl.pallas_call(functools.partial(whole_step, sz, layers, names), out_shap...  194 us
    pallas_call x1, Pallas kernels, deliver(): pl.pallas_call(functools.partial(deliver_kernel, count), out_shape=tuple(...  4.26 us

profile of v2, /device:TPU:0, one launch (start us, length us, event | category | flops | bytes accessed | tf_op | source)
XLA Modules:
  0.0 199.4 jit_solution(14447156793745012620)
XLA Ops:
  0.6 194.3 %whole_step.1 = (f32[512,512]{1,0:T(8,128)}, f32[512,512]{1,0:T(8,128)}, f32[2,128,384]{2,1,0:T(8,128)}, f32[2,3072]{1,0:T(2,128)}, f32[2,64,256]{2,1,0:T(8,128)...) custom-call(bf16[512,512]{1,0:T(8,128)(2,1)} %bitcast.7, ...), custom_call_target="tpu_custom_call" | custom-call | tf_op jit(solution)/shard_map/whole_step/pallas_call | solution.py:1595
  194.9 4.3 %deliver.1 = (f32[512,512]{1,0:T(8,128)}, f32[512,512]{1,0:T(8,128)}, f32[2,128,384]{2,1,0:T(8,128)}, f32[2,3072]{1,0:T(2,128)}, f32[2,64,256]{2,1,0:T(8,128)}, ...) custom-call(f32[512,512]{1,0:T(8,128)} %get-tuple-element.30.refs_0_, ...), custom_call_target="tpu_custom_call" | custom-call | tf_op jit(solution)/shard_map/deliver/pallas_call | solution.py:1633

commit v3 on v2

--- a/solution.py
+++ b/solution.py
@@ -38,6 +38,10 @@
         return carry
 
     return lax.fori_loop(0, count // unroll, turn, start)
+
+
+def odds(zf, zi):
+    return jnp.exp(jnp.minimum(-zf, 86.0)), jnp.exp(jnp.minimum(-zi, 86.0))
 
 
 def gate_weights(a, b):
@@ -87,7 +91,7 @@
     lax.fori_loop(0, rows // step, one, 0)
 
 
-def norm_back(stream, gain, grad, through, out, gain_sum, rows, step):
+def norm_back(stream, gain, grad, through, out, gain_sum, rows, step, low=None):
     width = stream.shape[1]
 
     def one(i, total):
@@ -97,7 +101,10 @@
         n = x * r
         g = grad[at, :]
         a = g * gain[...]
-        out[at, :] = through[at, :] + r * (a - n * jnp.mean(a * n, axis=-1, keepdims=True))
+        value = through[at, :] + r * (a - n * jnp.mean(a * n, axis=-1, keepdims=True))
+        out[at, :] = value
+        if low is not None:
+            low[at, :] = value.astype(BF16)
         return total + jnp.sum((g * n).reshape(step // 8, 8, width), axis=0)
 
     gain_sum[...] = lax.fori_loop(0, rows // step, one, jnp.zeros((8, width), F32))
@@ -675,7 +682,11 @@
 SENDS = 16
 STAGES = 5
 WINDOW = 4
+DELAY = 1.5
 SMALL = 1280
+
+
+ORDERS = (((0, 2, 1, 3), (1, 2, 0, 3)),) * 16
 
 
 class Units:
@@ -687,8 +698,7 @@
         core, x = section % 2, section // 2
         y, za, zb = batch % 2, (batch // 2) % 2, batch // 4
         self.core = core
-        self.bits = ((x, za, y, zb), (y, za, x, zb))
-        self.names = (("x", "za", "y", "zb"), ("y", "za", "x", "zb"))
+        self.where = (x, y, za, zb)
         self.partner = {
             "core": {"section": section + 1 - 2 * core},
             "x": {"section": section + 2 - 4 * x},
@@ -700,7 +710,6 @@
         self.links = ("core", "x", "y", "z")
         self.free_at = dict.fromkeys(self.links, 0.0)
         self.flying = dict.fromkeys(self.links, 0)
-        self.window = dict.fromkeys(self.links, WINDOW)
         self.queues = {link: [] for link in self.links}
         self.ready = {}
         self.summed = set()
@@ -708,20 +717,26 @@
         self.small_left = None
 
     def greet(self):
-        barrier = pltpu.get_barrier_semaphore()
         section = lax.axis_index("section")
         others = [self.partner["y"], self.partner["za"], self.partner["zb"]]
         others += [{"section": lax.rem(section + hop, 4)} for hop in range(1, 4)]
         for other in others:
-            pl.semaphore_signal(barrier, inc=1, device_id=other, device_id_type=MESH)
-        pl.semaphore_wait(barrier, len(others))
-
-    def name(self, stage, half):
-        return "core" if stage == 0 else self.names[half][stage - 1]
-
-    def link(self, stage, half):
-        name = self.name(stage, half)
+            pl.semaphore_signal(
+                pltpu.get_barrier_semaphore(), inc=1, device_id=other, device_id_type=MESH
+            )
+
+    def greeted(self):
+        pl.semaphore_wait(pltpu.get_barrier_semaphore(), 6)
+
+    def name(self, unit, stage, half):
+        return "core" if stage == 0 else ("x", "y", "za", "zb")[ORDERS[unit][half][stage - 1]]
+
+    def link(self, unit, stage, half):
+        name = self.name(unit, stage, half)
         return "z" if name[0] == "z" else name
+
+    def bit(self, unit, stage, half):
+        return self.where[ORDERS[unit][half][stage - 1]]
 
     def arrival(self, unit, stage, half):
         ref = self.arrived[stage].at[unit % RINGS[stage]]
@@ -734,13 +749,13 @@
         else:
             count = 16 >> stage
             src = self.arrived[stage - 1].at[unit % RINGS[stage - 1], half]
-            src = src.at[pl.ds((1 - self.bits[half][stage - 1]) * count, count)]
+            src = src.at[pl.ds((1 - self.bit(unit, stage, half)) * count, count)]
         return pltpu.make_async_remote_copy(
             src_ref=src,
             dst_ref=self.arrival(unit, stage, half),
             send_sem=self.send_sems.at[unit % SENDS, at],
             recv_sem=self.recv_sems.at[unit % RINGS[stage], at],
-            device_id=self.partner[self.name(stage, half)],
+            device_id=self.partner[self.name(unit, stage, half)],
             device_id_type=MESH,
         )
 
@@ -753,17 +768,18 @@
         return (before, min(stage + 1, STAGES - 1), half) in self.summed
 
     def credit(self, unit, stage, half):
-        if unit + RINGS[stage] < self.count:
+        after = unit + RINGS[stage]
+        if after < self.count:
             pl.semaphore_signal(
-                self.credits.at[0 if stage == 0 else 2 * stage - 1 + half],
+                self.credits.at[0 if stage == 0 else 2 * stage - 1 + half, after],
                 inc=1,
-                device_id=self.partner[self.name(stage, half)],
+                device_id=self.partner[self.name(after, stage, half)],
                 device_id_type=MESH,
             )
 
     def pump(self):
         for link, queue in self.queues.items():
-            while self.flying[link] < self.window[link]:
+            while self.flying[link] < WINDOW:
                 key = next((key for key in queue if self.has_place(*key)), None)
                 if key is None:
                     break
@@ -772,7 +788,7 @@
                 unit, stage, half = key
                 if unit >= RINGS[stage]:
                     at = 0 if stage == 0 else 2 * stage - 1 + half
-                    pl.semaphore_wait(self.credits.at[at], 1)
+                    pl.semaphore_wait(self.credits.at[at, unit], 1)
                 self.copies[key] = self.copy(*key)
                 self.copies[key].start()
                 blocks = 32 if stage == 0 else 16 >> stage
@@ -781,14 +797,10 @@
     def expect(self, link, size):
         rate = 250e3 if link == "core" else 45e3
         self.free_at[link] = max(self.now, self.free_at[link]) + size / rate
-        return self.free_at[link] + 1.5
-
-    def hold(self, link, window):
-        self.window[link] = window
-        self.pump()
+        return self.free_at[link] + DELAY
 
     def push(self, unit, stage, half):
-        self.queues[self.link(stage, half)].append((unit, stage, half))
+        self.queues[self.link(unit, stage, half)].append((unit, stage, half))
         self.pump()
 
     def produced(self, us, *which):
@@ -813,7 +825,6 @@
     def step(self, unit, stage, half):
         key = (unit, stage, half)
         del self.ready[key]
-        assert unit == 0 or (unit - 1, stage, half) in self.summed
         self.copies[key].wait_recv()
         here = self.arrival(unit, stage, half)
         if stage == 0:
@@ -822,10 +833,10 @@
         else:
             count = 16 >> stage
             before = self.arrived[stage - 1].at[unit % RINGS[stage - 1], half]
-            self.add(here, before.at[pl.ds(self.bits[half][stage - 1] * count, count)], count)
+            self.add(here, before.at[pl.ds(self.bit(unit, stage, half) * count, count)], count)
             self.copies.pop(key).wait_send()
         self.summed.add(key)
-        self.flying[self.link(stage, half)] -= 1
+        self.flying[self.link(unit, stage, half)] -= 1
         self.now += 0.25
         if stage > 1 or (unit, 1, 1 - half) in self.summed:
             if stage > 0:
@@ -922,8 +933,10 @@
             self.copies.pop(key).wait_send()
 
 
-def place(half, x, y, za, zb):
-    return (x * 8 + za * 4 + y * 2 + zb) if half == 0 else (y * 8 + za * 4 + x * 2 + zb)
+def place(unit, half, x, y, z):
+    where = (x, y, z % 2, z // 2)
+    order = ORDERS[unit][half]
+    return where[order[0]] * 8 + where[order[1]] * 4 + where[order[2]] * 2 + where[order[3]]
 
 
 def strided(start, steps):
@@ -941,10 +954,10 @@
     natural = r.natural
     last = layers - 1
     half = sz.hidden // 2
-    z0, z1 = ga.at[:, :768], r.z1
-    drive = r.p.at[:, : sz.hidden]
+    zs = (ga.at[:, :256], r.z1)
+    drive = ga
     homes = dict(gate_w=r.gate_hbm, out_w=r.out_hbm, up_w=r.up_hbm, down_w=r.down_hbm)
-    homes.update(u=r.u_save, a=r.a_save, b=r.b_save, zc=r.zc_save, states=r.states_save)
+    homes.update(u=r.u_save, zf=r.zf_save, zi=r.zi_save, zc=r.zc_save, states=r.states_save)
     homes.update(y1=r.y1_save, v=r.v_save, p=r.p_save, gb=r.gb_save, stream=r.stream_save)
     keys = types.SimpleNamespace(**{name: name for name in homes})
     index_of = {name: i for i, name in enumerate(homes)}
@@ -1065,14 +1078,13 @@
         part_enter(slots, prefix, enter, sz, reverse, parts[part])
 
     def in_turn(count, dots, rest, after=None):
-        zs = (z0, z1)
-        over(sz.rows // 256, lambda i: dots(0, zs[0], i))
+        over(sz.rows // 256, lambda i: dots(0, i))
         for n in range(count):
 
             def both(i):
                 if n + 1 < count:
-                    dots(n + 1, zs[(n + 1) % 2], i)
-                rest(n, zs[n % 2], i)
+                    dots(n + 1, i)
+                rest(n, i)
 
             over(sz.rows // 256, both)
             if after is not None:
@@ -1095,37 +1107,28 @@
         if layer == 0:
             save(layer, keys.stream, gx)
         need(keys.gate_w)
-        settled(keys.a, keys.b, keys.zc, keys.p)
+        settled(keys.zf, keys.zi, keys.zc)
         hw = 256
         bias = r.gate_bias
 
-        def gate_dots(n, z, i):
-            rows = tile(i, 256)
-            for part in range(3):
+        def gate_dots(n, i):
+            rows, to = tile(i, 256), slice(n * hw, (n + 1) * hw)
+            for part, z in enumerate((r.zf, r.zi, r.zc)):
                 cols = slice(part * sz.hidden + n * hw, part * sz.hidden + (n + 1) * hw)
-                z[rows, part * hw : (part + 1) * hw] = (
+                z[rows, to] = (
                     jnp.dot(r.u[rows, :], r.gate_w[:, cols], preferred_element_type=F32)
                     + bias[layer : layer + 1, cols]
                 )
 
-        def gate_rest(n, z, i):
+        def gate_rest(n, i):
             for chunk in range(4):
                 at = pl.ds(pl.multiple_of(i * 256 + chunk * 64, 64), 64)
                 vm, km = valid[at, :], keep[at, :]
                 for lane in range(hw // LANES):
-                    zf, zi, zc = (
-                        z[at, part * hw + lane * LANES : part * hw + (lane + 1) * LANES]
-                        for part in range(3)
-                    )
-                    dst = slice(n * hw + lane * LANES, n * hw + (lane + 1) * LANES)
-                    a = jnp.exp(jnp.minimum(-zf, 86.0))
-                    b = jnp.exp(jnp.minimum(-zi, 86.0))
-                    fp, ip, _ = gate_weights(a, b)
-                    decay[at, dst] = fp * km
-                    drive[at, dst] = ip * zc * vm
-                    r.a[at, dst] = a
-                    r.b[at, dst] = b
-                    r.zc[at, dst] = zc
+                    cols = slice(n * hw + lane * LANES, n * hw + (lane + 1) * LANES)
+                    fp, ip, _ = gate_weights(*odds(r.zf[at, cols], r.zi[at, cols]))
+                    decay[at, cols] = fp * km
+                    drive[at, cols] = ip * r.zc[at, cols] * vm
                     r.forget[...] += jnp.sum((fp * vm).reshape(8, 8, LANES), axis=0)
 
         flights = []
@@ -1145,6 +1148,8 @@
             r.chunk_p[:, lanes] = pair[0]
             r.chunk_t[:, lanes] = pair[1]
             part_totals(r.chunk_p, r.chunk_t, sz, False, prefix, mine, lanes)
+            if layer == 0 and n == 1:
+                units.greeted()
             flights.append(exchange_start(0, layer, n // 2))
 
         r.forget[...] = jnp.zeros_like(r.forget)
@@ -1152,11 +1157,11 @@
         small[0, layer * 4 : layer * 4 + 1, sz.hidden : sz.hidden + LANES] = jnp.sum(
             r.forget[...], axis=0, keepdims=True
         )
-        for name in (keys.a, keys.b, keys.zc):
+        for name in (keys.zf, keys.zi, keys.zc):
             save(layer, name)
         if layer < last:
             load(layer + 1, keys.gate_w)
-        settled(keys.states, keys.y1, keys.v, keys.gb, keys.stream)
+        settled(keys.states, keys.y1, keys.v, keys.p, keys.gb, keys.stream)
         states = r.states
         for part, lanes in enumerate(parts):
             exchange_end(*flights[part], False, part)
@@ -1170,6 +1175,8 @@
                 return h
 
             steps_of(sz.steps, 4, walk, enter[:, lanes])
+            if (layer, part) == (0, 0):
+                keep_cotangent()
         save(layer, keys.states)
         need(keys.out_w)
 
@@ -1187,18 +1194,17 @@
         save(layer, keys.v)
         need(keys.up_w)
 
-        def up_dots(n, z, i):
-            rows = tile(i, 256)
-            z[rows, :256] = jnp.dot(
-                r.v[rows, :], r.up_w[:, n * 256 : (n + 1) * 256], preferred_element_type=F32
+        def up_dots(n, i):
+            rows, cols = tile(i, 256), slice(n * 256, (n + 1) * 256)
+            r.p[rows, cols] = jnp.dot(
+                r.v[rows, :], r.up_w[:, cols], preferred_element_type=F32
             )
 
-        def up_rest(n, z, i):
+        def up_rest(n, i):
             cols = slice(n * 256, (n + 1) * 256)
             for chunk in range(4):
                 at = pl.ds(pl.multiple_of(i * 256 + chunk * 64, 64), 64)
-                p = z[at, :256]
-                r.p[at, cols] = p
+                p = r.p[at, cols]
                 r.gb[at, cols] = (p * normal_below(p)).astype(BF16)
 
         in_turn(sz.inner // 256, up_dots, up_rest)
@@ -1230,8 +1236,8 @@
             value = jnp.dot(low_t[...], r.gb[:, tile(n, 256)], preferred_element_type=F32)
             for b in range(8):
                 for h in range(2):
-                    at = place(h, s // 2, b % 2, (b // 2) % 2, b // 4)
-                    held[(unit + t) % HELD, s % 2, h, at] = value[
+                    at = [place(unit + k, h, s // 2, b % 2, b // 2) for k in range(2)]
+                    held[(unit + t) % HELD, s % 2, h, jnp.where(t == 0, *at)] = value[
                         b * 64 : b * 64 + 64, h * 128 : h * 128 + 128
                     ]
 
@@ -1245,8 +1251,14 @@
 
         over(sz.rows // 64, one)
 
-    def contract(left, weight, dst, count):
+    def turn_rows(src, dst, n):
+        at = tile(n, 128)
+        dst[:, at] = src[at, :].T
+
+    def contract(left, weight, dst, count, beside=None):
         def one(n):
+            if beside is not None:
+                beside(n)
             cols = tile(n, 256)
             dst[:, cols] = lax.dot_general(
                 left[...], weight[cols, :], (((1,), (1,)), ((), ())), preferred_element_type=F32
@@ -1255,8 +1267,6 @@
         over(count // 256, one)
 
     def up_grad(layer, unit):
-        need(keys.v)
-        wide_t[...] = r.v[...].T
         for k in range(2):
             units.room(unit + k)
 
@@ -1264,8 +1274,8 @@
             value = jnp.dot(wide_t[...], gp[:, tile(b, 256)], preferred_element_type=F32)
             for s in range(4):
                 for h in range(2):
-                    at = place(h, s // 2, b % 2, (b // 2) % 2, b // 4)
                     for t in range(2):
+                        at = place(unit + t, h, s // 2, b % 2, b // 2)
                         held[(unit + t) % HELD, s % 2, h, at] = value[
                             s * 128 + h * 64 : s * 128 + h * 64 + 64, t * 128 : t * 128 + 128
                         ]
@@ -1279,14 +1289,13 @@
 
         if layer < last:
             over(sz.steps, cast_state)
-        low_t[...] = low[...].T
         units.room(unit)
 
         def one(s):
-            value = jnp.dot(low_t[...], hb[:, tile(s, 256)], preferred_element_type=F32)
+            value = jnp.dot(r.go_t[...], hb[:, tile(s, 256)], preferred_element_type=F32)
             for b in range(8):
                 for h in range(2):
-                    at = place(h, s // 2, b % 2, (b // 2) % 2, b // 4)
+                    at = place(unit, h, s // 2, b % 2, b // 2)
                     held[unit % HELD, s % 2, h, at] = value[
                         b * 64 : b * 64 + 64, h * 128 : h * 128 + 128
                     ]
@@ -1302,52 +1311,55 @@
                 for name in which:
                     load(layer - 1, name)
 
-        if late:
-            cast(gx, low)
-            low_t[...] = low[...].T
-            units.passed(1)
-        else:
+        if not late:
             freed(keys.gb)
-        need(keys.down_w, keys.p)
-
-        def act_dots(n, z, i):
+        need(keys.down_w, keys.p, keys.v)
+
+        def act_dots(n, i):
             rows = tile(i, 256)
-            z[rows, :256] = lax.dot_general(
+            zs[n % 2][rows, :] = lax.dot_general(
                 low[rows, :],
                 r.down_w[n * 256 : (n + 1) * 256, :],
                 (((1,), (1,)), ((), ())),
                 preferred_element_type=F32,
             )
 
-        def act_rest(n, z, i):
+        def act_rest(n, i):
+            if n < 2:
+                turn_rows(r.v, wide_t, 2 * n + i)
+            elif n < 4 and late:
+                turn_rows(low, low_t, 2 * (n - 2) + i)
             cols = slice(n * 256, (n + 1) * 256)
             for chunk in range(4):
                 at = pl.ds(pl.multiple_of(i * 256 + chunk * 64, 64), 64)
                 p = r.p[at, cols]
                 slope = normal_below(p) + ROOT_TAU * p * jnp.exp(-0.5 * p * p)
-                gp[at, cols] = (z[at, :256] * slope).astype(BF16)
+                gp[at, cols] = (zs[n % 2][at, :] * slope).astype(BF16)
 
         in_turn(sz.inner // 256, act_dots, act_rest, lambda n: units.passed(0.6))
-        freed(keys.down_w, keys.p)
+        freed(keys.down_w, keys.p, keys.v)
         if not late:
             up_grad(layer, unit + 2)
-            freed(keys.v)
-        need(keys.up_w, keys.y1)
-        contract(gp, r.up_w, grad, sz.width)
+        need(keys.up_w, keys.y1, keys.u)
+
+        def turn_u(n):
+            for k in range(2):
+                turn_rows(r.u, r.u_t, 2 * n + k)
+
+        contract(gp, r.up_w, grad, sz.width, turn_u)
+        freed(keys.u)
         freed(keys.up_w)
         units.passed(1.5)
-        norm_back(r.y1, r.mlp_gain.at[layer : layer + 1], grad, gx, gy1, r.mlp_sum, sz.rows, 64)
+        norm_back(r.y1, r.mlp_gain.at[layer : layer + 1], grad, gx, gy1, r.mlp_sum, sz.rows, 64, low)
         freed(keys.y1)
-        cast(gy1, low)
         need(keys.states)
         units.passed(2)
-        units.hold("x", 1)
+        need(keys.out_w, keys.zf, keys.zi)
+        contract(low, r.out_w, ga, sz.hidden, lambda n: turn_rows(low, r.go_t, n))
+        freed(keys.out_w)
+        units.passed(1)
         if not late:
             out_grad(layer, unit + 4)
-        need(keys.out_w, keys.a, keys.b)
-        contract(low, r.out_w, ga, sz.hidden)
-        freed(keys.out_w)
-        units.passed(1)
         flights = []
         for part, lanes in enumerate(parts):
 
@@ -1355,7 +1367,7 @@
                 at = tile(j, sz.group)
                 if layer < last:
                     mask = jnp.concatenate([keep[at, :]] * (half // LANES), axis=1)
-                    d = gate_weights(r.a[at, lanes], r.b[at, lanes])[0] * mask
+                    d = gate_weights(*odds(r.zf[at, lanes], r.zi[at, lanes]))[0] * mask
                     decay[at, lanes] = d
                 else:
                     d = decay[at, lanes]
@@ -1368,8 +1380,6 @@
             part_totals(r.chunk_p, r.chunk_t, sz, True, prefix, mine, lanes)
             flights.append(exchange_start(1, layer, part))
             carried = [units.expect(link, 16384) for link in ("core", "x", "x")]
-            if part:
-                units.hold("x", WINDOW)
             units.passed(0.8)
         need(keys.zc)
         if late:
@@ -1389,7 +1399,7 @@
                 at = tile(j, sz.group)
                 d = decay[at, lanes]
                 q = ga[at, lanes] + m
-                a, b, zc = r.a[at, lanes], r.b[at, lanes], r.zc[at, lanes]
+                (a, b), zc = odds(r.zf[at, lanes], r.zi[at, lanes]), r.zc[at, lanes]
                 vm = jnp.concatenate([valid[at, :]] * 2, axis=1)
                 km = jnp.concatenate([keep[at, :]] * 2, axis=1)
                 fp, ip, inv = gate_weights(a, b)
@@ -1419,20 +1429,17 @@
             exchange_end(*flights[part], True, part)
             over(turns, lambda n: gate_lanes(n + part * turns))
             units.passed(1.8)
-        freed(keys.a, keys.b, keys.zc, keys.states)
-        need(keys.u)
-        wide_t[...] = r.u[...].T
-        freed(keys.u)
+        freed(keys.zf, keys.zi, keys.zc, keys.states)
         for k in range(2):
             units.room(unit + k)
 
         def gate_grad(b):
             cols = pl.ds(pl.multiple_of(b * 384, 128), 256)
-            value = jnp.dot(wide_t[...], gz[:, cols], preferred_element_type=F32)
+            value = jnp.dot(r.u_t[...], gz[:, cols], preferred_element_type=F32)
             for s in range(4):
                 for h in range(2):
-                    at = place(h, s // 2, b % 2, (b // 2) % 2, b // 4)
                     for t in range(2):
+                        at = place(unit + t, h, s // 2, b % 2, b // 2)
                         held[(unit + t) % HELD, s % 2, h, at] = value[
                             s * 128 + h * 64 : s * 128 + h * 64 + 64, t * 128 : t * 128 + 128
                         ]
@@ -1450,11 +1457,11 @@
                 ],
                 axis=1,
             )
-            value = jnp.dot(wide_t[...], right, preferred_element_type=F32)
+            value = jnp.dot(r.u_t[...], right, preferred_element_type=F32)
             for s in range(4):
                 for h in range(2):
                     for y in range(2):
-                        at = place(h, s // 2, y, z % 2, z // 2)
+                        at = place(unit, h, s // 2, y, z)
                         held[unit % HELD, s % 2, h, at] = value[
                             s * 128 + h * 64 : s * 128 + h * 64 + 64, y * 128 : y * 128 + 128
                         ]
@@ -1466,7 +1473,7 @@
         contract(gz, r.gate_w, grad, sz.width)
         freed(keys.gate_w)
         units.passed(2.5)
-        norm_back(r.stream, r.mix_gain.at[layer : layer + 1], grad, gy1, gx, r.mix_sum, sz.rows, 64)
+        norm_back(r.stream, r.mix_gain.at[layer : layer + 1], grad, gy1, gx, r.mix_sum, sz.rows, 64, low)
         freed(keys.stream)
         row = slice(layer * 4 + 3, layer * 4 + 4)
         small[0, row, : sz.width] = jnp.sum(r.mix_sum[...], axis=0, keepdims=True)
@@ -1474,7 +1481,6 @@
         units.passed(1.5)
 
     forward(0)
-    keep_cotangent()
     for layer in range(1, layers):
         forward(layer)
     out_copies = from_steps(gy1, r.layer_out, r.out_sems)
@@ -1531,8 +1537,8 @@
     results = len(outputs)
     kept = dict(
         u=((rows, d), BF16),
-        a=((rows, h), F32),
-        b=((rows, h), F32),
+        zf=((rows, h), F32),
+        zi=((rows, h), F32),
         zc=((rows, h), F32),
         states=((rows + sz.group, h), F32),
         y1=((rows, d), F32),
@@ -1556,8 +1562,10 @@
         low=vm(rows, d, kind=BF16),
         low_t=vm(d, rows, kind=BF16),
         wide_t=vm(d, rows, kind=BF16),
+        u_t=vm(d, rows, kind=BF16),
+        go_t=vm(d, rows, kind=BF16),
         hb=vm(rows, h, kind=BF16),
-        z1=vm(rows, 768),
+        z1=vm(rows, 256),
         forget=vm(8, LANES),
         ga=vm(rows, h),
         gz=vm(rows, 3 * h, kind=BF16),
@@ -1585,7 +1593,7 @@
         pair_recv=sems.DMA((2, layers, 2, sz.sections - 1)),
         send_sems=sems.DMA((SENDS, 2 * STAGES - 1)),
         recv_sems=sems.DMA((max(RINGS), 2 * STAGES - 1)),
-        credits=sems.REGULAR((2 * STAGES - 1,)),
+        credits=sems.REGULAR((2 * STAGES - 1, 8 * layers)),
         small_send=sems.DMA((STAGES,)),
         small_recv=sems.DMA((STAGES,)),
     )

time: 200 us -> 201 us (level)
  no operation moved by 1% of the time
where the time goes in v3:
time: 201 us; the launch traced here: 200 us
  Pallas kernels  200 us (100%)
    pallas_call x1, Pallas kernels, run_whole_step(): pl.pallas_call(functools.partial(whole_step, sz, layers, names), out_shap...  195 us
    pallas_call x1, Pallas kernels, deliver(): pl.pallas_call(functools.partial(deliver_kernel, count), out_shape=tuple(...  4.26 us

profile of v3, /device:TPU:0, one launch (start us, length us, event | category | flops | bytes accessed | tf_op | source)
XLA Modules:
  0.0 200.4 jit_solution(8846241277902157104)
XLA Ops:
  0.6 195.3 %whole_step.1 = (f32[512,512]{1,0:T(8,128)}, f32[512,512]{1,0:T(8,128)}, f32[2,128,384]{2,1,0:T(8,128)}, f32[2,3072]{1,0:T(2,128)}, f32[2,64,256]{2,1,0:T(8,128)...) custom-call(bf16[512,512]{1,0:T(8,128)(2,1)} %bitcast.7, ...), custom_call_target="tpu_custom_call" | custom-call | tf_op jit(solution)/shard_map/whole_step/pallas_call | solution.py:1603
  196.0 4.3 %deliver.1 = (f32[512,512]{1,0:T(8,128)}, f32[512,512]{1,0:T(8,128)}, f32[2,128,384]{2,1,0:T(8,128)}, f32[2,3072]{1,0:T(2,128)}, f32[2,64,256]{2,1,0:T(8,128)}, ...) custom-call(f32[512,512]{1,0:T(8,128)} %get-tuple-element.30.refs_0_, ...), custom_call_target="tpu_custom_call" | custom-call | tf_op jit(solution)/shard_map/deliver/pallas_call | solution.py:1641

commit v4 on v3

--- a/solution.py
+++ b/solution.py
@@ -567,7 +567,7 @@
 
 VMEM = pl.BlockSpec(memory_space=pltpu.VMEM)
 ANY = pl.BlockSpec(memory_space=pl.ANY)
-LIMIT = 62 * 2**20
+LIMIT = 63 * 2**20
 
 
 def shape(*dims, kind=F32):
@@ -678,7 +678,7 @@
 
 BLOCK = 64
 HELD = 3
-RINGS = (4, 5, 6, 16, 16)
+RINGS = (4, 5, 5, 16, 16)
 SENDS = 16
 STAGES = 5
 WINDOW = 4
@@ -954,10 +954,10 @@
     natural = r.natural
     last = layers - 1
     half = sz.hidden // 2
-    zs = (ga.at[:, :256], r.z1)
-    drive = ga
+    zs = (ga.at[:, :768], r.z1)
+    drive = r.drive
     homes = dict(gate_w=r.gate_hbm, out_w=r.out_hbm, up_w=r.up_hbm, down_w=r.down_hbm)
-    homes.update(u=r.u_save, zf=r.zf_save, zi=r.zi_save, zc=r.zc_save, states=r.states_save)
+    homes.update(u=r.u_save, a=r.a_save, b=r.b_save, zc=r.zc_save, states=r.states_save)
     homes.update(y1=r.y1_save, v=r.v_save, p=r.p_save, gb=r.gb_save, stream=r.stream_save)
     keys = types.SimpleNamespace(**{name: name for name in homes})
     index_of = {name: i for i, name in enumerate(homes)}
@@ -1107,15 +1107,15 @@
         if layer == 0:
             save(layer, keys.stream, gx)
         need(keys.gate_w)
-        settled(keys.zf, keys.zi, keys.zc)
+        settled(keys.a, keys.b, keys.zc)
         hw = 256
         bias = r.gate_bias
 
         def gate_dots(n, i):
-            rows, to = tile(i, 256), slice(n * hw, (n + 1) * hw)
-            for part, z in enumerate((r.zf, r.zi, r.zc)):
+            rows = tile(i, 256)
+            for part in range(3):
                 cols = slice(part * sz.hidden + n * hw, part * sz.hidden + (n + 1) * hw)
-                z[rows, to] = (
+                zs[n % 2][rows, part * hw : (part + 1) * hw] = (
                     jnp.dot(r.u[rows, :], r.gate_w[:, cols], preferred_element_type=F32)
                     + bias[layer : layer + 1, cols]
                 )
@@ -1125,10 +1125,18 @@
                 at = pl.ds(pl.multiple_of(i * 256 + chunk * 64, 64), 64)
                 vm, km = valid[at, :], keep[at, :]
                 for lane in range(hw // LANES):
+                    zf, zi, zc = (
+                        zs[n % 2][at, part * hw + lane * LANES : part * hw + (lane + 1) * LANES]
+                        for part in range(3)
+                    )
                     cols = slice(n * hw + lane * LANES, n * hw + (lane + 1) * LANES)
-                    fp, ip, _ = gate_weights(*odds(r.zf[at, cols], r.zi[at, cols]))
+                    a, b = odds(zf, zi)
+                    fp, ip, _ = gate_weights(a, b)
                     decay[at, cols] = fp * km
-                    drive[at, cols] = ip * r.zc[at, cols] * vm
+                    drive[at, cols] = ip * zc * vm
+                    r.a[at, cols] = a
+                    r.b[at, cols] = b
+                    r.zc[at, cols] = zc
                     r.forget[...] += jnp.sum((fp * vm).reshape(8, 8, LANES), axis=0)
 
         flights = []
@@ -1157,7 +1165,7 @@
         small[0, layer * 4 : layer * 4 + 1, sz.hidden : sz.hidden + LANES] = jnp.sum(
             r.forget[...], axis=0, keepdims=True
         )
-        for name in (keys.zf, keys.zi, keys.zc):
+        for name in (keys.a, keys.b, keys.zc):
             save(layer, name)
         if layer < last:
             load(layer + 1, keys.gate_w)
@@ -1196,7 +1204,7 @@
 
         def up_dots(n, i):
             rows, cols = tile(i, 256), slice(n * 256, (n + 1) * 256)
-            r.p[rows, cols] = jnp.dot(
+            zs[n % 2][rows, :256] = jnp.dot(
                 r.v[rows, :], r.up_w[:, cols], preferred_element_type=F32
             )
 
@@ -1204,7 +1212,8 @@
             cols = slice(n * 256, (n + 1) * 256)
             for chunk in range(4):
                 at = pl.ds(pl.multiple_of(i * 256 + chunk * 64, 64), 64)
-                p = r.p[at, cols]
+                p = zs[n % 2][at, :256]
+                r.p[at, cols] = p
                 r.gb[at, cols] = (p * normal_below(p)).astype(BF16)
 
         in_turn(sz.inner // 256, up_dots, up_rest)
@@ -1317,7 +1326,7 @@
 
         def act_dots(n, i):
             rows = tile(i, 256)
-            zs[n % 2][rows, :] = lax.dot_general(
+            zs[n % 2][rows, :256] = lax.dot_general(
                 low[rows, :],
                 r.down_w[n * 256 : (n + 1) * 256, :],
                 (((1,), (1,)), ((), ())),
@@ -1334,7 +1343,7 @@
                 at = pl.ds(pl.multiple_of(i * 256 + chunk * 64, 64), 64)
                 p = r.p[at, cols]
                 slope = normal_below(p) + ROOT_TAU * p * jnp.exp(-0.5 * p * p)
-                gp[at, cols] = (zs[n % 2][at, :] * slope).astype(BF16)
+                gp[at, cols] = (zs[n % 2][at, :256] * slope).astype(BF16)
 
         in_turn(sz.inner // 256, act_dots, act_rest, lambda n: units.passed(0.6))
         freed(keys.down_w, keys.p, keys.v)
@@ -1354,7 +1363,7 @@
         freed(keys.y1)
         need(keys.states)
         units.passed(2)
-        need(keys.out_w, keys.zf, keys.zi)
+        need(keys.out_w, keys.a, keys.b)
         contract(low, r.out_w, ga, sz.hidden, lambda n: turn_rows(low, r.go_t, n))
         freed(keys.out_w)
         units.passed(1)
@@ -1367,7 +1376,7 @@
                 at = tile(j, sz.group)
                 if layer < last:
                     mask = jnp.concatenate([keep[at, :]] * (half // LANES), axis=1)
-                    d = gate_weights(*odds(r.zf[at, lanes], r.zi[at, lanes]))[0] * mask
+                    d = gate_weights(r.a[at, lanes], r.b[at, lanes])[0] * mask
                     decay[at, lanes] = d
                 else:
                     d = decay[at, lanes]
@@ -1399,7 +1408,7 @@
                 at = tile(j, sz.group)
                 d = decay[at, lanes]
                 q = ga[at, lanes] + m
-                (a, b), zc = odds(r.zf[at, lanes], r.zi[at, lanes]), r.zc[at, lanes]
+                a, b, zc = r.a[at, lanes], r.b[at, lanes], r.zc[at, lanes]
                 vm = jnp.concatenate([valid[at, :]] * 2, axis=1)
                 km = jnp.concatenate([keep[at, :]] * 2, axis=1)
                 fp, ip, inv = gate_weights(a, b)
@@ -1429,7 +1438,7 @@
             exchange_end(*flights[part], True, part)
             over(turns, lambda n: gate_lanes(n + part * turns))
             units.passed(1.8)
-        freed(keys.zf, keys.zi, keys.zc, keys.states)
+        freed(keys.a, keys.b, keys.zc, keys.states)
         for k in range(2):
             units.room(unit + k)
 
@@ -1537,8 +1546,8 @@
     results = len(outputs)
     kept = dict(
         u=((rows, d), BF16),
-        zf=((rows, h), F32),
-        zi=((rows, h), F32),
+        a=((rows, h), F32),
+        b=((rows, h), F32),
         zc=((rows, h), F32),
         states=((rows + sz.group, h), F32),
         y1=((rows, d), F32),
@@ -1565,7 +1574,8 @@
         u_t=vm(d, rows, kind=BF16),
         go_t=vm(d, rows, kind=BF16),
         hb=vm(rows, h, kind=BF16),
-        z1=vm(rows, 256),
+        z1=vm(rows, 768),
+        drive=vm(rows, h),
         forget=vm(8, LANES),
         ga=vm(rows, h),
         gz=vm(rows, 3 * h, kind=BF16),

time: 201 us -> 201 us (level)
  no operation moved by 1% of the time
where the time goes in v4:
time: 201 us; the launch traced here: 200 us
  Pallas kernels  200 us (100%)
    pallas_call x1, Pallas kernels, run_whole_step(): pl.pallas_call(functools.partial(whole_step, sz, layers, names), out_shap...  195 us
    pallas_call x1, Pallas kernels, deliver(): pl.pallas_call(functools.partial(deliver_kernel, count), out_shape=tuple(...  4.26 us

profile of v4, /device:TPU:0, one launch (start us, length us, event | category | flops | bytes accessed | tf_op | source)
XLA Modules:
  0.0 200.4 jit_solution(14354198211728224407)
XLA Ops:
  0.6 195.3 %whole_step.1 = (f32[512,512]{1,0:T(8,128)}, f32[512,512]{1,0:T(8,128)}, f32[2,128,384]{2,1,0:T(8,128)}, f32[2,3072]{1,0:T(2,128)}, f32[2,64,256]{2,1,0:T(8,128)...) custom-call(bf16[512,512]{1,0:T(8,128)(2,1)} %bitcast.7, ...), custom_call_target="tpu_custom_call" | custom-call | tf_op jit(solution)/shard_map/whole_step/pallas_call | solution.py:1613
  195.9 4.3 %deliver.1 = (f32[512,512]{1,0:T(8,128)}, f32[512,512]{1,0:T(8,128)}, f32[2,128,384]{2,1,0:T(8,128)}, f32[2,3072]{1,0:T(2,128)}, f32[2,64,256]{2,1,0:T(8,128)}, ...) custom-call(f32[512,512]{1,0:T(8,128)} %get-tuple-element.30.refs_0_, ...), custom_call_target="tpu_custom_call" | custom-call | tf_op jit(solution)/shard_map/deliver/pallas_call | solution.py:1651

commit v5 on v4

--- a/solution.py
+++ b/solution.py
@@ -934,7 +934,10 @@
 
 
 def place(unit, half, x, y, z):
-    where = (x, y, z % 2, z // 2)
+    return spot(unit, half, (x, y, z % 2, z // 2))
+
+
+def spot(unit, half, where):
     order = ORDERS[unit][half]
     return where[order[0]] * 8 + where[order[1]] * 4 + where[order[2]] * 2 + where[order[3]]
 
@@ -1001,9 +1004,7 @@
     len_load = pltpu.make_async_copy(r.lengths, r.lens, r.in_sems.at[2])
     len_load.start()
     act_load.start()
-    for name in (keys.gate_w, keys.out_w, keys.up_w, keys.down_w):
-        load(0, name)
-    cot_load.start()
+    load(0, keys.gate_w)
     units.greet()
     mine[...] = jnp.zeros_like(mine)
     small[0] = jnp.zeros((8, SMALL), F32)
@@ -1077,13 +1078,15 @@
             copy.wait()
         part_enter(slots, prefix, enter, sz, reverse, parts[part])
 
-    def in_turn(count, dots, rest, after=None):
+    def in_turn(count, dots, rest, after=None, third=None):
         over(sz.rows // 256, lambda i: dots(0, i))
         for n in range(count):
 
             def both(i):
                 if n + 1 < count:
                     dots(n + 1, i)
+                if third is not None and n > 0:
+                    third(n - 1, i)
                 rest(n, i)
 
             over(sz.rows // 256, both)
@@ -1107,6 +1110,10 @@
         if layer == 0:
             save(layer, keys.stream, gx)
         need(keys.gate_w)
+        if layer == 0:
+            for name in (keys.out_w, keys.up_w, keys.down_w):
+                load(0, name)
+            cot_load.start()
         settled(keys.a, keys.b, keys.zc)
         hw = 256
         bias = r.gate_bias
@@ -1202,27 +1209,51 @@
         save(layer, keys.v)
         need(keys.up_w)
 
+        tiles = range(8) if layer < last else (0, 2, 4, 6, 1, 3, 5, 7)
+
         def up_dots(n, i):
-            rows, cols = tile(i, 256), slice(n * 256, (n + 1) * 256)
+            rows, cols = tile(i, 256), slice(tiles[n] * 256, (tiles[n] + 1) * 256)
             zs[n % 2][rows, :256] = jnp.dot(
                 r.v[rows, :], r.up_w[:, cols], preferred_element_type=F32
             )
 
         def up_rest(n, i):
-            cols = slice(n * 256, (n + 1) * 256)
+            cols = slice(tiles[n] * 256, (tiles[n] + 1) * 256)
             for chunk in range(4):
                 at = pl.ds(pl.multiple_of(i * 256 + chunk * 64, 64), 64)
                 p = zs[n % 2][at, :256]
                 r.p[at, cols] = p
                 r.gb[at, cols] = (p * normal_below(p)).astype(BF16)
 
-        in_turn(sz.inner // 256, up_dots, up_rest)
+        def down_part(n, i):
+            s, unit = tiles[n] // 2, tiles[n] % 2
+            value = jnp.dot(
+                low_t[tile(i, 256), :],
+                r.gb[:, tiles[n] * 256 : (tiles[n] + 1) * 256],
+                preferred_element_type=F32,
+            )
+            for k in range(4):
+                for h in range(2):
+                    at = spot(unit, h, (s // 2, k % 2, k // 2, i))
+                    held[unit, s % 2, h, at] = value[
+                        k * 64 : k * 64 + 64, h * 128 : h * 128 + 128
+                    ]
+
+        def up_after(n):
+            units.passed(0.3)
+            if n == 4:
+                units.produced(0, 0)
+
+        if layer < last:
+            in_turn(8, up_dots, up_rest)
+        else:
+            in_turn(8, up_dots, up_rest, up_after, down_part)
+            over(2, lambda i: down_part(7, i))
+            units.produced(0.2, 1)
         save(layer, keys.p)
         save(layer, keys.gb)
         if layer < last:
             load(layer + 1, keys.up_w)
-        else:
-            down_grad(layer, 0)
         need(keys.down_w)
         out = r.stream if layer < last else gy1
 

time: 201 us -> 199 us (0.990)
  no operation moved by 1% of the time
where the time goes in v5:
time: 199 us
  Pallas kernels  198 us (99%)
    pallas_call x1, Pallas kernels, run_whole_step(): pl.pallas_call(functools.partial(whole_step, sz, layers, names), out_shap...  194 us
    pallas_call x1, Pallas kernels, deliver(): pl.pallas_call(functools.partial(deliver_kernel, count), out_shape=tuple(...  4.26 us

profile of v5, /device:TPU:0, one launch (start us, length us, event | category | flops | bytes accessed | tf_op | source)
XLA Modules:
  0.0 199.0 jit_solution(16036425203374399062)
XLA Ops:
  0.6 194.0 %whole_step.1 = (f32[512,512]{1,0:T(8,128)}, f32[512,512]{1,0:T(8,128)}, f32[2,128,384]{2,1,0:T(8,128)}, f32[2,3072]{1,0:T(2,128)}, f32[2,64,256]{2,1,0:T(8,128)...) custom-call(bf16[512,512]{1,0:T(8,128)(2,1)} %bitcast.7, ...), custom_call_target="tpu_custom_call" | custom-call | tf_op jit(solution)/shard_map/whole_step/pallas_call | solution.py:1644
  194.6 4.3 %deliver.1 = (f32[512,512]{1,0:T(8,128)}, f32[512,512]{1,0:T(8,128)}, f32[2,128,384]{2,1,0:T(8,128)}, f32[2,3072]{1,0:T(2,128)}, f32[2,64,256]{2,1,0:T(8,128)}, ...) custom-call(f32[512,512]{1,0:T(8,128)} %get-tuple-element.30.refs_0_, ...), custom_call_target="tpu_custom_call" | custom-call | tf_op jit(solution)/shard_map/deliver/pallas_call | solution.py:1682

commit v6 on v5

--- a/solution.py
+++ b/solution.py
@@ -686,7 +686,12 @@
 SMALL = 1280
 
 
-ORDERS = (((0, 2, 1, 3), (1, 2, 0, 3)),) * 16
+EVEN = ((0, 2, 1, 3), (1, 2, 0, 3))
+PLANE = ((0, 1, 2, 3), (1, 0, 2, 3))
+ORDERS = [EVEN] * 16
+ORDERS[0] = ((0, 2, 1, 3), (2, 1, 3, 0))
+ORDERS[1] = ((1, 2, 0, 3), (0, 2, 1, 3))
+ORDERS[6] = ORDERS[9] = PLANE
 
 
 class Units:
@@ -715,6 +720,7 @@
         self.summed = set()
         self.copies = {}
         self.small_left = None
+        self.leaving = []
 
     def greet(self):
         section = lax.axis_index("section")
@@ -847,7 +853,7 @@
         elif stage < STAGES - 1:
             self.push(unit, stage + 1, half)
         else:
-            self.finish(unit, half, here[0])
+            self.finish(unit, half, here.at[0])
             self.credit(unit, stage, half)
         self.pump()
 
@@ -855,11 +861,14 @@
         layer, k = self.count // 8 - 1 - unit // 8, unit % 8
         if k < 2 or k == 4:
             ref, at = (self.down_weight_grad, k) if k < 2 else (self.out_weight_grad, 0)
-            ref[layer, :, at * 256 + half * 128 : at * 256 + half * 128 + 128] = block
+            to = ref.at[layer, :, at * 256 + half * 128 : at * 256 + half * 128 + 128]
         else:
             ref, at = (self.up_weight_grad, k - 2) if k < 4 else (self.gate_weight_grad, k - 5)
             rows = slice(half * BLOCK, half * BLOCK + BLOCK)
-            ref[layer, rows, at * LANES : at * LANES + LANES] = block
+            to = ref.at[layer, rows, at * LANES : at * LANES + LANES]
+        copy = pltpu.make_async_copy(block, to, self.result_sems.at[unit, half])
+        copy.start()
+        self.leaving.append(copy)
 
     def small_copy(self, stage):
         name = ("core", "x", "y", "za", "zb")[stage]
@@ -890,6 +899,7 @@
         else:
             for copy in self.small_copies:
                 copy.wait_send()
+            self.small_done()
 
     def open(self, unit, stage, half):
         halves = range(2) if stage == 0 else (half,)
@@ -931,6 +941,8 @@
             self.take(item)
         for key in list(self.copies):
             self.copies.pop(key).wait_send()
+        for copy in self.leaving:
+            copy.wait()
 
 
 def place(unit, half, x, y, z):
@@ -1073,9 +1085,16 @@
         slots[me, :, lanes] = mine[:, lanes]
         return slots, copies
 
+    sent = {}
+
+    def sends_settled(part):
+        for copy in sent.pop(part, ()):
+            copy.wait_send()
+
     def exchange_end(slots, copies, reverse, part):
         for copy in copies:
-            copy.wait()
+            copy.wait_recv()
+        sent[part] = copies
         part_enter(slots, prefix, enter, sz, reverse, parts[part])
 
     def in_turn(count, dots, rest, after=None, third=None):
@@ -1162,6 +1181,7 @@
             pair = steps_of(sz.steps, 2, totals, (one, jnp.zeros_like(one)))
             r.chunk_p[:, lanes] = pair[0]
             r.chunk_t[:, lanes] = pair[1]
+            sends_settled(n // 2)
             part_totals(r.chunk_p, r.chunk_t, sz, False, prefix, mine, lanes)
             if layer == 0 and n == 1:
                 units.greeted()
@@ -1417,6 +1437,7 @@
             pair = steps_of(sz.steps, 2, totals, (one, jnp.zeros_like(one)), reverse=True)
             r.chunk_p[:, lanes] = pair[0]
             r.chunk_t[:, lanes] = pair[1]
+            sends_settled(part)
             part_totals(r.chunk_p, r.chunk_t, sz, True, prefix, mine, lanes)
             flights.append(exchange_start(1, layer, part))
             carried = [units.expect(link, 16384) for link in ("core", "x", "x")]
@@ -1528,6 +1549,38 @@
     units.passed(2)
     for index, layer in enumerate(reversed(range(layers))):
         backward(layer, 8 * index)
+    def small_done():
+        total = small[STAGES]
+        count = jnp.int32(0)
+        for s in range(r.lens.shape[0]):
+            for d in range(r.lens.shape[1]):
+                count = count + r.lens[s, d]
+        scale = 1.0 / (count.astype(F32) * sz.hidden)
+        for layer in range(layers):
+            one = slice(layer, layer + 1)
+            for part in range(3):
+                r.bias_out[one, part * sz.hidden : (part + 1) * sz.hidden] = total[
+                    layer * 4 + part : layer * 4 + part + 1, : sz.hidden
+                ]
+            row = slice(layer * 4 + 3, layer * 4 + 4)
+            r.mix_out[one, :] = total[row, : sz.width]
+            r.mlp_out[one, :] = total[row, sz.width : 2 * sz.width]
+            lanes = total[layer * 4 : layer * 4 + 1, sz.hidden : sz.hidden + LANES]
+            r.forget_out[one, :] = jnp.sum(lanes, axis=1, keepdims=True) * scale + jnp.zeros(
+                (1, LANES), F32
+            )
+        pairs = (
+            (r.bias_out, r.gate_bias_grad),
+            (r.mix_out, r.mix_gain_grad),
+            (r.mlp_out, r.mlp_gain_grad),
+            (r.forget_out, r.forget_mean),
+        )
+        for k, (src, dst) in enumerate(pairs):
+            copy = pltpu.make_async_copy(src, dst, r.small_out_sems.at[k])
+            copy.start()
+            units.leaving.append(copy)
+
+    units.small_done = small_done
     units.small_start()
     for copy in out_copies:
         copy.wait()
@@ -1536,24 +1589,8 @@
     units.drain()
     for copy in out_copies:
         copy.wait()
-    total = small[STAGES]
-    count = jnp.int32(0)
-    for s in range(r.lens.shape[0]):
-        for d in range(r.lens.shape[1]):
-            count = count + r.lens[s, d]
-    scale = 1.0 / (count.astype(F32) * sz.hidden)
-    for layer in range(layers):
-        for part in range(3):
-            r.gate_bias_grad[layer : layer + 1, part * sz.hidden : (part + 1) * sz.hidden] = total[
-                layer * 4 + part : layer * 4 + part + 1, : sz.hidden
-            ]
-        row = slice(layer * 4 + 3, layer * 4 + 4)
-        r.mix_gain_grad[layer : layer + 1, :] = total[row, : sz.width]
-        r.mlp_gain_grad[layer : layer + 1, :] = total[row, sz.width : 2 * sz.width]
-        lanes = total[layer * 4 : layer * 4 + 1, sz.hidden : sz.hidden + LANES]
-        r.forget_mean[layer : layer + 1, :] = (
-            jnp.sum(lanes, axis=1, keepdims=True) * scale + jnp.zeros((1, LANES), F32)
-        )
+    for part in range(2):
+        sends_settled(part)
 
 
 def run_whole_step(sz, layers, named):
@@ -1565,14 +1602,14 @@
     outputs = dict(
         layer_out=(shape(rows, d), ANY),
         input_grad=(shape(rows, d), ANY),
-        gate_weight_grad=(shape(layers, 128, 384), VMEM),
-        gate_bias_grad=(shape(layers, 3 * h), VMEM),
-        out_weight_grad=(shape(layers, 64, 256), VMEM),
-        up_weight_grad=(shape(layers, 128, 256), VMEM),
-        down_weight_grad=(shape(layers, 64, 512), VMEM),
-        mix_gain_grad=(shape(layers, d), VMEM),
-        mlp_gain_grad=(shape(layers, d), VMEM),
-        forget_mean=(shape(layers, LANES), VMEM),
+        gate_weight_grad=(shape(layers, 128, 384), ANY),
+        gate_bias_grad=(shape(layers, 3 * h), ANY),
+        out_weight_grad=(shape(layers, 64, 256), ANY),
+        up_weight_grad=(shape(layers, 128, 256), ANY),
+        down_weight_grad=(shape(layers, 64, 512), ANY),
+        mix_gain_grad=(shape(layers, d), ANY),
+        mlp_gain_grad=(shape(layers, d), ANY),
+        forget_mean=(shape(layers, LANES), ANY),
     )
     results = len(outputs)
     kept = dict(
@@ -1625,6 +1662,12 @@
         small=vm(STAGES + 1, 8, SMALL),
         small_arrived=vm(STAGES, 8, SMALL),
         in_sems=sems.DMA((3,)),
+        bias_out=vm(layers, 3 * h),
+        mix_out=vm(layers, d),
+        mlp_out=vm(layers, d),
+        forget_out=vm(layers, LANES),
+        small_out_sems=sems.DMA((4,)),
+        result_sems=sems.DMA((8 * layers, 2)),
         lens=pltpu.SMEM(lengths.shape, jnp.int32),
         out_sems=sems.DMA((d // LANES,)),
         natural=vm(d // LANES, rows, LANES),

time: 199 us -> 200 us (level)
  no operation moved by 1% of the time
where the time goes in v6:
time: 200 us
  Pallas kernels  199 us (100%)
    pallas_call x1, Pallas kernels, run_whole_step(): pl.pallas_call(functools.partial(whole_step, sz, layers, names), out_shap...  195 us
    pallas_call x1, Pallas kernels, deliver(): pl.pallas_call(functools.partial(deliver_kernel, count), out_shape=tuple(...  4.26 us

profile of v6, /device:TPU:0, one launch (start us, length us, event | category | flops | bytes accessed | tf_op | source)
XLA Modules:
  0.0 199.7 jit_solution(3913710440914627969)
XLA Ops:
  0.6 194.6 %whole_step.1 = (f32[512,512]{1,0:T(8,128)}, f32[512,512]{1,0:T(8,128)}, f32[2,128,384]{2,1,0:T(8,128)}, f32[2,3072]{1,0:T(2,128)}, f32[2,64,256]{2,1,0:T(8,128)...) custom-call(bf16[512,512]{1,0:T(8,128)(2,1)} %bitcast.7, ...), custom_call_target="tpu_custom_call" | custom-call | tf_op jit(solution)/shard_map/whole_step/pallas_call | solution.py:1687
  195.2 4.3 %deliver.1 = (f32[512,512]{1,0:T(8,128)}, f32[512,512]{1,0:T(8,128)}, f32[2,128,384]{2,1,0:T(8,128)}, f32[2,3072]{1,0:T(2,128)}, f32[2,64,256]{2,1,0:T(8,128)}, ...) custom-call(f32[512,512]{1,0:T(8,128)} %get-tuple-element.30.refs_0_, ...), custom_call_target="tpu_custom_call" | custom-call | tf_op jit(solution)/shard_map/deliver/pallas_call | solution.py:1725

commit v7 on v6

--- a/solution.py
+++ b/solution.py
@@ -687,11 +687,7 @@
 
 
 EVEN = ((0, 2, 1, 3), (1, 2, 0, 3))
-PLANE = ((0, 1, 2, 3), (1, 0, 2, 3))
 ORDERS = [EVEN] * 16
-ORDERS[0] = ((0, 2, 1, 3), (2, 1, 3, 0))
-ORDERS[1] = ((1, 2, 0, 3), (0, 2, 1, 3))
-ORDERS[6] = ORDERS[9] = PLANE
 
 
 class Units:
@@ -745,16 +741,15 @@
         return self.where[ORDERS[unit][half][stage - 1]]
 
     def arrival(self, unit, stage, half):
-        ref = self.arrived[stage].at[unit % RINGS[stage]]
-        return ref if stage == 0 else ref.at[half]
+        return self.arrived[stage].at[unit % RINGS[stage], half]
 
     def copy(self, unit, stage, half):
-        at = 0 if stage == 0 else 2 * stage - 1 + half
+        at = 2 * stage + half
         if stage == 0:
-            src = self.held.at[unit % HELD, 1 - self.core]
+            src = self.held.at[unit % HELD, 1 - self.core, half]
         else:
             count = 16 >> stage
-            src = self.arrived[stage - 1].at[unit % RINGS[stage - 1], half]
+            src = self.arrival(unit, stage - 1, half)
             src = src.at[pl.ds((1 - self.bit(unit, stage, half)) * count, count)]
         return pltpu.make_async_remote_copy(
             src_ref=src,
@@ -767,17 +762,13 @@
 
     def has_place(self, unit, stage, half):
         before = unit - RINGS[stage]
-        if before < 0:
-            return True
-        if stage == 0:
-            return (before, 1, 0) in self.summed and (before, 1, 1) in self.summed
-        return (before, min(stage + 1, STAGES - 1), half) in self.summed
+        return before < 0 or (before, min(stage + 1, STAGES - 1), half) in self.summed
 
     def credit(self, unit, stage, half):
         after = unit + RINGS[stage]
         if after < self.count:
             pl.semaphore_signal(
-                self.credits.at[0 if stage == 0 else 2 * stage - 1 + half, after],
+                self.credits.at[2 * stage + half, after],
                 inc=1,
                 device_id=self.partner[self.name(after, stage, half)],
                 device_id_type=MESH,
@@ -793,12 +784,10 @@
                 self.flying[link] += 1
                 unit, stage, half = key
                 if unit >= RINGS[stage]:
-                    at = 0 if stage == 0 else 2 * stage - 1 + half
-                    pl.semaphore_wait(self.credits.at[at, unit], 1)
+                    pl.semaphore_wait(self.credits.at[2 * stage + half, unit], 1)
                 self.copies[key] = self.copy(*key)
                 self.copies[key].start()
-                blocks = 32 if stage == 0 else 16 >> stage
-                self.ready[key] = self.expect(link, blocks * BLOCK * LANES * 4)
+                self.ready[key] = self.expect(link, (16 >> stage) * BLOCK * LANES * 4)
 
     def expect(self, link, size):
         rate = 250e3 if link == "core" else 45e3
@@ -812,7 +801,8 @@
     def produced(self, us, *which):
         self.now += us
         for unit in which:
-            self.push(unit, 0, 0)
+            for half in range(2):
+                self.push(unit, 0, half)
         self.passed(0)
 
     def add(self, dst, src, count):
@@ -834,23 +824,18 @@
         self.copies[key].wait_recv()
         here = self.arrival(unit, stage, half)
         if stage == 0:
-            for h in range(2):
-                self.add(here.at[h], self.held.at[unit % HELD, self.core, h], 16)
+            self.add(here, self.held.at[unit % HELD, self.core, half], 16)
         else:
             count = 16 >> stage
-            before = self.arrived[stage - 1].at[unit % RINGS[stage - 1], half]
+            before = self.arrival(unit, stage - 1, half)
             self.add(here, before.at[pl.ds(self.bit(unit, stage, half) * count, count)], count)
             self.copies.pop(key).wait_send()
         self.summed.add(key)
         self.flying[self.link(unit, stage, half)] -= 1
         self.now += 0.25
-        if stage > 1 or (unit, 1, 1 - half) in self.summed:
-            if stage > 0:
-                self.credit(unit, stage - 1, half if stage > 1 else 0)
-        if stage == 0:
-            for h in range(2):
-                self.push(unit, 1, h)
-        elif stage < STAGES - 1:
+        if stage > 0:
+            self.credit(unit, stage - 1, half)
+        if stage < STAGES - 1:
             self.push(unit, stage + 1, half)
         else:
             self.finish(unit, half, here.at[0])
@@ -930,11 +915,12 @@
             self.take(item)
 
     def room(self, unit):
-        before = (unit - HELD, 0, 0)
-        while unit >= HELD and before not in self.summed:
-            self.take(self.next())
-        if before in self.copies:
-            self.copies.pop(before).wait_send()
+        for half in range(2):
+            before = (unit - HELD, 0, half)
+            while unit >= HELD and before not in self.summed:
+                self.take(self.next())
+            if before in self.copies:
+                self.copies.pop(before).wait_send()
 
     def drain(self):
         while item := self.next():
@@ -1215,13 +1201,7 @@
         save(layer, keys.states)
         need(keys.out_w)
 
-        def out_tile(n):
-            cols = tile(n, 256)
-            r.y1[:, cols] = stream[:, cols] + jnp.dot(
-                hb[...], r.out_w[:, cols], preferred_element_type=F32
-            )
-
-        over(sz.width // 256, out_tile)
+        r.y1[...] = stream[...] + jnp.dot(hb[...], r.out_w[...], preferred_element_type=F32)
         save(layer, keys.y1)
         if layer < last:
             load(layer + 1, keys.out_w)
@@ -1277,13 +1257,7 @@
         need(keys.down_w)
         out = r.stream if layer < last else gy1
 
-        def down_tile(n):
-            cols = tile(n, 256)
-            out[:, cols] = r.y1[:, cols] + jnp.dot(
-                r.gb[...], r.down_w[:, cols], preferred_element_type=F32
-            )
-
-        over(sz.width // 256, down_tile)
+        out[...] = r.y1[...] + jnp.dot(r.gb[...], r.down_w[...], preferred_element_type=F32)
         if layer < last:
             load(layer + 1, keys.down_w)
 
@@ -1675,9 +1649,9 @@
         save_sems=sems.DMA((len(kept) + 4,)),
         pair_send=sems.DMA((2, layers, 2, sz.sections - 1)),
         pair_recv=sems.DMA((2, layers, 2, sz.sections - 1)),
-        send_sems=sems.DMA((SENDS, 2 * STAGES - 1)),
-        recv_sems=sems.DMA((max(RINGS), 2 * STAGES - 1)),
-        credits=sems.REGULAR((2 * STAGES - 1, 8 * layers)),
+        send_sems=sems.DMA((SENDS, 2 * STAGES)),
+        recv_sems=sems.DMA((max(RINGS), 2 * STAGES)),
+        credits=sems.REGULAR((2 * STAGES, 8 * layers)),
         small_send=sems.DMA((STAGES,)),
         small_recv=sems.DMA((STAGES,)),
     )
@@ -1701,12 +1675,18 @@
 def deliver_kernel(count, *refs):
     sources, targets, held = refs[:count], refs[count : 2 * count], refs[2 * count : 3 * count - 1]
     sems = refs[3 * count - 1]
-    arrivals = [
-        pltpu.make_async_copy(sources[i], held[i], sems.at[0, i]) for i in range(count - 1)
-    ]
-    departures = [
-        pltpu.make_async_copy(held[i], targets[i], sems.at[1, i]) for i in range(count - 1)
-    ]
+    arrivals, departures = [], []
+    for i in range(count - 1):
+        pieces = 4 if len(held[i].shape) == 2 and held[i].shape[0] >= 256 else 1
+        size = held[i].shape[0] // pieces
+        for k in range(pieces):
+            at, sem = pl.ds(k * size, size), 4 * i + k
+            arrivals.append(
+                pltpu.make_async_copy(sources[i].at[at], held[i].at[at], sems.at[0, sem])
+            )
+            departures.append(
+                pltpu.make_async_copy(held[i].at[at], targets[i].at[at], sems.at[1, sem])
+            )
     for copy in arrivals:
         copy.start()
     for layer in range(targets[-1].shape[0]):
@@ -1728,7 +1708,7 @@
         in_specs=[ANY] * (count - 1) + [scalars],
         out_specs=[ANY] * (count - 1) + [scalars],
         scratch_shapes=[pltpu.VMEM(value.shape, F32) for value in values[:-1]]
-        + [pltpu.SemaphoreType.DMA((2, count - 1))],
+        + [pltpu.SemaphoreType.DMA((2, 4 * count))],
         compiler_params=pltpu.CompilerParams(vmem_limit_bytes=LIMIT),
         name="deliver",
     )(*values)

time: 200 us -> 202 us (1.010)
    pallas_call x1, Pallas kernels: 195 us -> 197 us  [run_whole_step(): pl.pallas_call(functools.partial(whole_step, sz, layers, names), out_shap...]
where the time goes in v7:
time: 202 us
  Pallas kernels  201 us (100%)
    pallas_call x1, Pallas kernels, run_whole_step(): pl.pallas_call(functools.partial(whole_step, sz, layers, names), out_shap...  197 us
    pallas_call x1, Pallas kernels, deliver(): pl.pallas_call(functools.partial(deliver_kernel, count), out_shape=tuple(...  4.53 us

profile of v7, /device:TPU:0, one launch (start us, length us, event | category | flops | bytes accessed | tf_op | source)
XLA Modules:
  0.0 202.1 jit_solution(12878152318040965250)
XLA Ops:
  0.6 196.8 %whole_step.1 = (f32[512,512]{1,0:T(8,128)}, f32[512,512]{1,0:T(8,128)}, f32[2,128,384]{2,1,0:T(8,128)}, f32[2,3072]{1,0:T(2,128)}, f32[2,64,256]{2,1,0:T(8,128)...) custom-call(bf16[512,512]{1,0:T(8,128)(2,1)} %bitcast.7, ...), custom_call_target="tpu_custom_call" | custom-call | tf_op jit(solution)/shard_map/whole_step/pallas_call | solution.py:1661
  197.4 4.5 %deliver.1 = (f32[512,512]{1,0:T(8,128)}, f32[512,512]{1,0:T(8,128)}, f32[2,128,384]{2,1,0:T(8,128)}, f32[2,3072]{1,0:T(2,128)}, f32[2,64,256]{2,1,0:T(8,128)}, ...) custom-call(f32[512,512]{1,0:T(8,128)} %get-tuple-element.30.refs_0_, ...), custom_call_target="tpu_custom_call" | custom-call | tf_op jit(solution)/shard_map/deliver/pallas_call | solution.py:1705

commit v8 on v6

--- a/solution.py
+++ b/solution.py
@@ -687,11 +687,7 @@
 
 
 EVEN = ((0, 2, 1, 3), (1, 2, 0, 3))
-PLANE = ((0, 1, 2, 3), (1, 0, 2, 3))
 ORDERS = [EVEN] * 16
-ORDERS[0] = ((0, 2, 1, 3), (2, 1, 3, 0))
-ORDERS[1] = ((1, 2, 0, 3), (0, 2, 1, 3))
-ORDERS[6] = ORDERS[9] = PLANE
 
 
 class Units:
@@ -1098,17 +1094,13 @@
         part_enter(slots, prefix, enter, sz, reverse, parts[part])
 
     def in_turn(count, dots, rest, after=None, third=None):
-        over(sz.rows // 256, lambda i: dots(0, i))
+        dots(0)
         for n in range(count):
-
-            def both(i):
-                if n + 1 < count:
-                    dots(n + 1, i)
-                if third is not None and n > 0:
-                    third(n - 1, i)
-                rest(n, i)
-
-            over(sz.rows // 256, both)
+            if n + 1 < count:
+                dots(n + 1)
+            if third is not None and n > 0:
+                third(n - 1)
+            rest(n)
             if after is not None:
                 after(n)
 
@@ -1137,18 +1129,17 @@
         hw = 256
         bias = r.gate_bias
 
-        def gate_dots(n, i):
-            rows = tile(i, 256)
+        def gate_dots(n):
             for part in range(3):
                 cols = slice(part * sz.hidden + n * hw, part * sz.hidden + (n + 1) * hw)
-                zs[n % 2][rows, part * hw : (part + 1) * hw] = (
-                    jnp.dot(r.u[rows, :], r.gate_w[:, cols], preferred_element_type=F32)
+                zs[n % 2][:, part * hw : (part + 1) * hw] = (
+                    jnp.dot(r.u[...], r.gate_w[:, cols], preferred_element_type=F32)
                     + bias[layer : layer + 1, cols]
                 )
 
-        def gate_rest(n, i):
-            for chunk in range(4):
-                at = pl.ds(pl.multiple_of(i * 256 + chunk * 64, 64), 64)
+        def gate_rest(n):
+            for chunk in range(sz.rows // 64):
+                at = slice(chunk * 64, chunk * 64 + 64)
                 vm, km = valid[at, :], keep[at, :]
                 for lane in range(hw // LANES):
                     zf, zi, zc = (
@@ -1215,13 +1206,7 @@
         save(layer, keys.states)
         need(keys.out_w)
 
-        def out_tile(n):
-            cols = tile(n, 256)
-            r.y1[:, cols] = stream[:, cols] + jnp.dot(
-                hb[...], r.out_w[:, cols], preferred_element_type=F32
-            )
-
-        over(sz.width // 256, out_tile)
+        r.y1[...] = stream[...] + jnp.dot(hb[...], r.out_w[...], preferred_element_type=F32)
         save(layer, keys.y1)
         if layer < last:
             load(layer + 1, keys.out_w)
@@ -1231,30 +1216,30 @@
 
         tiles = range(8) if layer < last else (0, 2, 4, 6, 1, 3, 5, 7)
 
-        def up_dots(n, i):
-            rows, cols = tile(i, 256), slice(tiles[n] * 256, (tiles[n] + 1) * 256)
-            zs[n % 2][rows, :256] = jnp.dot(
-                r.v[rows, :], r.up_w[:, cols], preferred_element_type=F32
+        def up_dots(n):
+            cols = slice(tiles[n] * 256, (tiles[n] + 1) * 256)
+            zs[n % 2][:, :256] = jnp.dot(
+                r.v[...], r.up_w[:, cols], preferred_element_type=F32
             )
 
-        def up_rest(n, i):
+        def up_rest(n):
             cols = slice(tiles[n] * 256, (tiles[n] + 1) * 256)
-            for chunk in range(4):
-                at = pl.ds(pl.multiple_of(i * 256 + chunk * 64, 64), 64)
+            for chunk in range(sz.rows // 64):
+                at = slice(chunk * 64, chunk * 64 + 64)
                 p = zs[n % 2][at, :256]
                 r.p[at, cols] = p
                 r.gb[at, cols] = (p * normal_below(p)).astype(BF16)
 
-        def down_part(n, i):
+        def down_part(n):
             s, unit = tiles[n] // 2, tiles[n] % 2
             value = jnp.dot(
-                low_t[tile(i, 256), :],
+                low_t[...],
                 r.gb[:, tiles[n] * 256 : (tiles[n] + 1) * 256],
                 preferred_element_type=F32,
             )
-            for k in range(4):
+            for k in range(8):
                 for h in range(2):
-                    at = spot(unit, h, (s // 2, k % 2, k // 2, i))
+                    at = place(unit, h, s // 2, k % 2, k // 2)
                     held[unit, s % 2, h, at] = value[
                         k * 64 : k * 64 + 64, h * 128 : h * 128 + 128
                     ]
@@ -1268,7 +1253,7 @@
             in_turn(8, up_dots, up_rest)
         else:
             in_turn(8, up_dots, up_rest, up_after, down_part)
-            over(2, lambda i: down_part(7, i))
+            down_part(7)
             units.produced(0.2, 1)
         save(layer, keys.p)
         save(layer, keys.gb)
@@ -1277,13 +1262,7 @@
         need(keys.down_w)
         out = r.stream if layer < last else gy1
 
-        def down_tile(n):
-            cols = tile(n, 256)
-            out[:, cols] = r.y1[:, cols] + jnp.dot(
-                r.gb[...], r.down_w[:, cols], preferred_element_type=F32
-            )
-
-        over(sz.width // 256, down_tile)
+        out[...] = r.y1[...] + jnp.dot(r.gb[...], r.down_w[...], preferred_element_type=F32)
         if layer < last:
             load(layer + 1, keys.down_w)
 
@@ -1375,23 +1354,22 @@
             freed(keys.gb)
         need(keys.down_w, keys.p, keys.v)
 
-        def act_dots(n, i):
-            rows = tile(i, 256)
-            zs[n % 2][rows, :256] = lax.dot_general(
-                low[rows, :],
+        def act_dots(n):
+            zs[n % 2][:, :256] = lax.dot_general(
+                low[...],
                 r.down_w[n * 256 : (n + 1) * 256, :],
                 (((1,), (1,)), ((), ())),
                 preferred_element_type=F32,
             )
 
-        def act_rest(n, i):
-            if n < 2:
-                turn_rows(r.v, wide_t, 2 * n + i)
-            elif n < 4 and late:
-                turn_rows(low, low_t, 2 * (n - 2) + i)
+        def act_rest(n):
+            if n < 4:
+                turn_rows(r.v, wide_t, n)
+            elif late:
+                turn_rows(low, low_t, n - 4)
             cols = slice(n * 256, (n + 1) * 256)
-            for chunk in range(4):
-                at = pl.ds(pl.multiple_of(i * 256 + chunk * 64, 64), 64)
+            for chunk in range(sz.rows // 64):
+                at = slice(chunk * 64, chunk * 64 + 64)
                 p = r.p[at, cols]
                 slope = normal_below(p) + ROOT_TAU * p * jnp.exp(-0.5 * p * p)
                 gp[at, cols] = (zs[n % 2][at, :256] * slope).astype(BF16)

time: 200 us -> 188 us (0.940)
  Pallas kernels: 199 us -> 187 us
    pallas_call x1, Pallas kernels: 195 us -> 183 us  [run_whole_step(): pl.pallas_call(functools.partial(whole_step, sz, layers, names), out_shap...]
where the time goes in v8:
time: 188 us
  Pallas kernels  187 us (99%)
    pallas_call x1, Pallas kernels, run_whole_step(): pl.pallas_call(functools.partial(whole_step, sz, layers, names), out_shap...  183 us
    pallas_call x1, Pallas kernels, deliver(): pl.pallas_call(functools.partial(deliver_kernel, count), out_shape=tuple(...  4.26 us

profile of v8, /device:TPU:0, one launch (start us, length us, event | category | flops | bytes accessed | tf_op | source)
XLA Modules:
  0.0 187.6 jit_solution(11983615113296971511)
XLA Ops:
  0.6 182.5 %whole_step.1 = (f32[512,512]{1,0:T(8,128)}, f32[512,512]{1,0:T(8,128)}, f32[2,128,384]{2,1,0:T(8,128)}, f32[2,3072]{1,0:T(2,128)}, f32[2,64,256]{2,1,0:T(8,128)...) custom-call(bf16[512,512]{1,0:T(8,128)(2,1)} %bitcast.7, ...), custom_call_target="tpu_custom_call" | custom-call | tf_op jit(solution)/shard_map/whole_step/pallas_call | solution.py:1665
  183.2 4.3 %deliver.1 = (f32[512,512]{1,0:T(8,128)}, f32[512,512]{1,0:T(8,128)}, f32[2,128,384]{2,1,0:T(8,128)}, f32[2,3072]{1,0:T(2,128)}, f32[2,64,256]{2,1,0:T(8,128)}, ...) custom-call(f32[512,512]{1,0:T(8,128)} %get-tuple-element.30.refs_0_, ...), custom_call_target="tpu_custom_call" | custom-call | tf_op jit(solution)/shard_map/deliver/pallas_call | solution.py:1703

commit v9 on v8

--- a/solution.py
+++ b/solution.py
@@ -1019,6 +1019,13 @@
     len_load.wait()
     fill_masks(r.lens, valid, keep, sz, True)
 
+    def norm_straight(stream, gain, low):
+        for i in range(sz.rows // 64):
+            at = slice(i * 64, i * 64 + 64)
+            x = stream[at, :]
+            scale = lax.rsqrt(jnp.mean(x * x, axis=-1, keepdims=True) + epsilon)
+            low[at, :] = (x * scale * gain[...]).astype(BF16)
+
     def to_steps(src, put):
         def cast(i):
             at = tile(i, 64)
@@ -1034,7 +1041,11 @@
                 ]
                 put(tile(j, sz.group), slice(k * LANES, (k + 1) * LANES), jnp.concatenate(parts, axis=0))
 
-        over(sz.steps, gather)
+        def gather_four(i):
+            for k in range(4):
+                gather(i * 4 + k)
+
+        over(sz.steps // 4, gather_four)
 
     def from_steps(src, dst, sem):
         def scatter(j):
@@ -1116,7 +1127,7 @@
     def forward(layer):
         stream = r.stream if layer > 0 else gx
         settled(keys.u)
-        norm_rows(stream, r.mix_gain.at[layer : layer + 1], r.u, sz.rows, 128)
+        norm_straight(stream, r.mix_gain.at[layer : layer + 1], r.u)
         save(layer, keys.u)
         if layer == 0:
             save(layer, keys.stream, gx)
@@ -1169,7 +1180,7 @@
                 return pair[0] * d, pair[1] * d + drive[at, lanes]
 
             one = jnp.ones((sz.group, half), F32)
-            pair = steps_of(sz.steps, 2, totals, (one, jnp.zeros_like(one)))
+            pair = steps_of(sz.steps, 8, totals, (one, jnp.zeros_like(one)))
             r.chunk_p[:, lanes] = pair[0]
             r.chunk_t[:, lanes] = pair[1]
             sends_settled(n // 2)
@@ -1200,7 +1211,7 @@
                 hb[at, lanes] = h.astype(BF16)
                 return h
 
-            steps_of(sz.steps, 4, walk, enter[:, lanes])
+            steps_of(sz.steps, 8, walk, enter[:, lanes])
             if (layer, part) == (0, 0):
                 keep_cotangent()
         save(layer, keys.states)
@@ -1210,7 +1221,7 @@
         save(layer, keys.y1)
         if layer < last:
             load(layer + 1, keys.out_w)
-        norm_rows(r.y1, r.mlp_gain.at[layer : layer + 1], r.v, sz.rows, 128)
+        norm_straight(r.y1, r.mlp_gain.at[layer : layer + 1], r.v)
         save(layer, keys.v)
         need(keys.up_w)
 

time: 188 us -> 186 us (0.989)
  Pallas kernels: 187 us -> 185 us
    pallas_call x1, Pallas kernels: 183 us -> 180 us  [run_whole_step(): pl.pallas_call(functools.partial(whole_step, sz, layers, names), out_shap...]
where the time goes in v9:
time: 186 us; the launch traced here: 185 us
  Pallas kernels  185 us (99%)
    pallas_call x1, Pallas kernels, run_whole_step(): pl.pallas_call(functools.partial(whole_step, sz, layers, names), out_shap...  180 us
    pallas_call x1, Pallas kernels, deliver(): pl.pallas_call(functools.partial(deliver_kernel, count), out_shape=tuple(...  4.26 us

profile of v9, /device:TPU:0, one launch (start us, length us, event | category | flops | bytes accessed | tf_op | source)
XLA Modules:
  0.0 185.5 jit_solution(13578959107793532427)
XLA Ops:
  0.6 180.4 %whole_step.1 = (f32[512,512]{1,0:T(8,128)}, f32[512,512]{1,0:T(8,128)}, f32[2,128,384]{2,1,0:T(8,128)}, f32[2,3072]{1,0:T(2,128)}, f32[2,64,256]{2,1,0:T(8,128)...) custom-call(bf16[512,512]{1,0:T(8,128)(2,1)} %bitcast.7, ...), custom_call_target="tpu_custom_call" | custom-call | tf_op jit(solution)/shard_map/whole_step/pallas_call | solution.py:1676
  181.0 4.3 %deliver.1 = (f32[512,512]{1,0:T(8,128)}, f32[512,512]{1,0:T(8,128)}, f32[2,128,384]{2,1,0:T(8,128)}, f32[2,3072]{1,0:T(2,128)}, f32[2,64,256]{2,1,0:T(8,128)}, ...) custom-call(f32[512,512]{1,0:T(8,128)} %get-tuple-element.30.refs_0_, ...), custom_call_target="tpu_custom_call" | custom-call | tf_op jit(solution)/shard_map/deliver/pallas_call | solution.py:1714
